TPU v7x, 128 devices: a whole 4x4x4 slice. The times are simulated.
128 devices in a mesh: dom: 32 (over y, z_lo, x), orb: 4 (over z_hi, core).
Axes of the slice: x: 4, y: 4, z: 4 (z_hi: 2, z_lo: 2; z = z_hi * 2 + z_lo), core: 2. Of those that a mesh axis runs over, the one named last changes fastest.
Arguments:
- orbitals: float32 [32, 32, 32, 24, 128], P('orb', 'dom'), may hold values from -90 to 90
- potential: float32 [32, 32, 24, 128], P('dom'), may hold values from -1 to 0.5
Outputs:
- filtered: float32 [32, 32, 32, 24, 128], P('orb', 'dom')
- correlation: float32 [32, 32], replicated
- subspace: float32 [32, 32], replicated
All inputs are finite; a program needn't handle non-finite values.
Results may differ from a plain program's by a relative error of at most 0.0001.
Values sent between devices are 32-bit elements; how exact they have to be, the bound alone decides.
A program may use at most 128 MiB of HBM per device.

v0:
```python
import math

import jax
import jax.numpy as jnp
from jax import lax
from jax.sharding import PartitionSpec as P

HALO = 6


SPACING = 0.5
UPPER = 44.0
CUTOFF = 4.0
LOWEST = -1.0


def from_behind(block, axis, distance):
    devices = range(lax.axis_size(axis))
    route = [(i - distance, i) for i in devices if i - distance in devices]
    return lax.ppermute(block, axis, route)


def stencil_weights():
    weights = []
    for offset in range(1, HALO + 1):
        weights.append(
            2.0
            * (-1.0) ** (offset + 1)
            * math.factorial(HALO) ** 2
            / (offset * offset * math.factorial(HALO - offset) * math.factorial(HALO + offset))
        )
    return weights


def along(extended, axis_pos, length):
    weights = stencil_weights()
    center = lax.slice_in_dim(extended, HALO, HALO + length, axis=axis_pos)
    summed = -2.0 * sum(weights) * center
    for offset in range(1, HALO + 1):
        ahead = lax.slice_in_dim(extended, HALO + offset, HALO + offset + length, axis=axis_pos)
        behind = lax.slice_in_dim(extended, HALO - offset, HALO - offset + length, axis=axis_pos)
        summed = summed + weights[offset - 1] * (ahead + behind)
    return summed


def extend(values, axis_pos, stride, coord, count):
    length = values.shape[axis_pos]
    upper_face = lax.slice_in_dim(values, length - HALO, length, axis=axis_pos)
    lower_face = lax.slice_in_dim(values, 0, HALO, axis=axis_pos)
    received = []
    for moved, face in ((stride, upper_face), (-stride, lower_face)):
        received.append(from_behind(face, "dom", moved))
    below = jnp.where(coord > 0, received[0], 0.0)
    above = jnp.where(coord < count - 1, received[1], 0.0)
    return jnp.concatenate([below, values, above], axis=axis_pos)


def chebyshev(start, apply_fn):
    half_width = (UPPER - CUTOFF) / 2.0
    middle = (UPPER + CUTOFF) / 2.0
    sigma_now = half_width / (LOWEST - middle)
    gamma_value = 2.0 / sigma_now
    previous = start
    current = sigma_now / half_width * (apply_fn(start) - middle * start)
    sigma_next = 1.0 / (gamma_value - sigma_now)
    following = (
        2.0 * sigma_next / half_width * (apply_fn(current) - middle * current)
        - sigma_now * sigma_next * previous
    )
    previous, current, sigma_now = (current, following, sigma_next)
    return current


def gram_pair(left, right_one, right_two):
    first = jnp.dot(
        left, right_one.T, precision=lax.Precision.HIGHEST, preferred_element_type=jnp.float32
    )
    second = jnp.dot(
        left, right_two.T, precision=lax.Precision.HIGHEST, preferred_element_type=jnp.float32
    )
    return jnp.stack([first, second])


def shards(orbitals, potential):
    local_block = orbitals[:, 0]
    pot_local = potential[0]
    count_dom = lax.axis_size("dom")
    count_y = min(4, count_dom // 4)
    count_x = count_dom // (2 * count_y)
    position = lax.axis_index("dom")
    block_z = position % 2
    block_y = position // 2 % count_y
    block_x = position // (2 * count_y)

    def apply_ham(values):
        ext_x = extend(values, 1, 2 * count_y, block_x, count_x)
        ext_y = extend(values, 2, 2, block_y, count_y)
        ext_z = extend(values, 3, 1, block_z, 2)
        laplace = (
            along(ext_x, 1, values.shape[1])
            + along(ext_y, 2, values.shape[2])
            + along(ext_z, 3, values.shape[3])
        )
        return -0.5 / SPACING**2 * laplace + pot_local[None] * values

    result = chebyshev(local_block, apply_ham)
    image = apply_ham(result)
    total_cells = result.shape[1] * result.shape[2] * result.shape[3] * count_dom
    half_width = (UPPER - CUTOFF) / 2.0
    mine_y = result.reshape(result.shape[0], -1)
    mine_h = image.reshape(image.shape[0], -1)
    piece = lax.all_gather(result, "orb", axis=0, tiled=True)
    partial_cols = gram_pair(piece.reshape(piece.shape[0], -1), mine_y, mine_h)
    summed_cols = lax.psum(partial_cols, "dom")
    summed = lax.all_gather(summed_cols, "orb", axis=2, tiled=True)
    correlation = summed[0] / total_cells
    subspace = summed[1] / (total_cells * half_width)
    return (result[:, None], correlation, subspace)


def solution(mesh):
    placed = (P("orb", "dom", None, None, None), P("dom", None, None, None))
    return jax.shard_map(
        shards,
        mesh=mesh,
        in_specs=placed,
        out_specs=(P("orb", "dom", None, None, None), P(), P()),
        check_vma=False,
    )
```

profile of v0, /device:TPU:1, one launch (start us, length us, event | category | flops | bytes accessed | tf_op | source)
XLA Modules:
  0.0 525.1 jit_solution(9426059709726361574)
XLA Ops:
  7.2 3.7 copy.30
  10.9 3.8 fusion.342
  14.7 4.5 copy.10
  20.5 4.5 copy.12
  25.0 5.5 %collective-permute-start.5 = (f32[8,32,24,6]{1,2,3,0:T(8,128)}, f32[8,32,24,6]{1,2,3,0:T(8,128)}, u32[]{:S(2)}, u32[]{:S(2)}) collective-permute-start(f32[8,32,24,6]{1,2,3,0:T(8,128)} %copy.12), channel_id=1, source_target_pairs={{0,4},{4,8},{8,12},{12,16},{16,20},{20,24},{24,28},{28,32},{32,36}... | collective-permute-start | bytes 442376 | tf_op jit(solution)/shard_map/ppermute | solution.py:20
  31.9 5.0 collective-permute-start.3
  39.2 8.1 %collective-permute-start.1 = (f32[8,6,24,128]{3,0,2,1:T(8,128)}, f32[8,6,24,128]{3,0,2,1:T(8,128)}, u32[]{:S(2)}, u32[]{:S(2)}) collective-permute-start(f32[8,6,24,128]{3,0,2,1:T(8,128)} %get-tuple-element.24), channel_id=1, source_target_pairs={{0,32},{4,36},{8,40},{12,44},{16,48},{20,52},{24,56},{28,60},{32,6... | collective-permute-start | bytes 1769480 | tf_op jit(solution)/shard_map/ppermute | solution.py:20
  48.1 1.7 collective-permute-start
  49.9 5.2 copy.11
  55.1 5.2 copy.13
  60.3 4.1 broadcast_select_fusion.5
  64.4 1.9 broadcast_select_fusion.4
  67.1 1.9 broadcast_select_fusion.17
  70.0 9.2 %collective-permute-done.2 = f32[8,32,6,128]{3,0,2,1:T(8,128)} collective-permute-done((f32[8,32,6,128]{3,0,2,1:T(8,128)}, f32[8,32,6,128]{3,0,2,1:T(8,128)}, u32[]{:S(2)}, u32[]{:S(2)}) %collective-permute-start.2) | collective-permute-done | bytes 786464 | tf_op jit(solution)/shard_map/ppermute | solution.py:20
  79.2 2.1 broadcast_select_fusion.11
  81.3 34.3 %broadcast_multiply_fusion = (f32[8,32,24,128]{3,0,2,1:T(8,128)}, f32[8,32,24,128]{3,0,2,1:T(8,128)}) fusion(f32[8,32,24,128]{3,0,2,1:T(8,128)S(1)} %bitcast.33, f32[32,24,128]{2,1,0:T(8,128)S(1)} %bitcast.34, f32[8,32,24,6]{3,0,2,1:T(8,128)} %broadcast_select_fusion.4, f32[8,32,24,6]{3,0,2,1:T(8,128)} %broadcast_select_fusion.5, ...), kind=kLoop, calls=%fused_computation.476 | loop fusion | flops 77856768 | bytes 12877824 | tf_op jit(solution)/shard_map/mul | solution.py:64
  115.6 6.7 %fusion.337 = (f32[8,32,24,6]{3,0,2,1:T(8,128)}, f32[8,32,24,6]{3,0,2,1:T(8,128)}) fusion(f32[8,32,24,128]{3,0,2,1:T(8,128)} %get-tuple-element.9), kind=kLoop, calls=%fused_computation.524 | loop fusion | bytes 589824 | tf_op jit(solution)/shard_map/slice | solution.py:49
  123.5 4.5 copy.16
  128.0 2.1 collective-permute-start.11
  130.1 4.5 copy.14
  135.8 9.9 %collective-permute-start.9 = (f32[8,32,6,128]{3,0,2,1:T(8,128)}, f32[8,32,6,128]{3,0,2,1:T(8,128)}, u32[]{:S(2)}, u32[]{:S(2)}) collective-permute-start(f32[8,32,6,128]{3,0,2,1:T(8,128)} %get-tuple-element.20), channel_id=1, source_target_pairs={{0,8},{4,12},{8,16},{12,20},{16,24},{20,28},{24,32},{28,36},{32,40... | collective-permute-start | bytes 2359304 | tf_op jit(solution)/shard_map/ppermute | solution.py:20
  149.4 27.1 %collective-permute-start.7 = (f32[8,6,24,128]{3,0,2,1:T(8,128)}, f32[8,6,24,128]{3,0,2,1:T(8,128)}, u32[]{:S(2)}, u32[]{:S(2)}) collective-permute-start(f32[8,6,24,128]{3,0,2,1:T(8,128)} %get-tuple-element.22), channel_id=1, source_target_pairs={{0,32},{4,36},{8,40},{12,44},{16,48},{20,52},{24,56},{28,60},{32,6... | collective-permute-start | bytes 1769480 | tf_op jit(solution)/shard_map/ppermute | solution.py:20
  176.5 5.2 copy.17
  181.8 5.2 copy.15
  187.0 2.0 broadcast_select_fusion.2
  190.0 1.9 broadcast_select_fusion.3
  191.9 1.9 broadcast_select_fusion.15
  195.8 2.1 broadcast_select_fusion.9
  197.9 36.2 %fusion.52 = f32[8,32,24,128]{3,0,2,1:T(8,128)} fusion(f32[8,32,24,128]{3,0,2,1:T(8,128)S(1)} %copy-done.1, f32[8,6,24,128]{3,0,2,1:T(8,128)} %broadcast_select_fusion.14, f32[8,6,24,128]{3,0,2,1:T(8,128)} %broadcast_select_fusion.15, f32[8,32,6,128]{3,0,2,1:T(8,128)} %broadcast_select_fusion.8, f32[8,32,6,128]{3,0,2,1:T(8,128)} %broadcast_select_fusion.9, ...), kind=kLoop, calls=%fused_computation.222 | loop fusion | flops 79429632 | bytes 16023552 | tf_op jit(solution)/shard_map/sub | solution.py:67
  234.2 1.9 copy-done
  236.0 3.8 fusion.334
  239.8 4.5 copy.20
  244.3 10.6 %collective-permute-start.17 = (f32[8,32,24,6]{1,2,3,0:T(8,128)}, f32[8,32,24,6]{1,2,3,0:T(8,128)}, u32[]{:S(2)}, u32[]{:S(2)}) collective-permute-start(f32[8,32,24,6]{1,2,3,0:T(8,128)} %copy.20), channel_id=1, source_target_pairs={{0,4},{4,8},{8,12},{12,16},{16,20},{20,24},{24,28},{28,32},{32,36}... | collective-permute-start | bytes 442376 | tf_op jit(solution)/shard_map/ppermute | solution.py:20
  255.0 4.5 copy.18
  262.0 4.5 collective-permute-start.15
  268.9 28.2 %collective-permute-start.13 = (f32[8,6,24,128]{3,0,2,1:T(8,128)}, f32[8,6,24,128]{3,0,2,1:T(8,128)}, u32[]{:S(2)}, u32[]{:S(2)}) collective-permute-start(f32[8,6,24,128]{3,0,2,1:T(8,128)} %get-tuple-element.16), channel_id=1, source_target_pairs={{0,32},{4,36},{8,40},{12,44},{16,48},{20,52},{24,56},{28,60},{32,6... | collective-permute-start | bytes 1769480 | tf_op jit(solution)/shard_map/ppermute | solution.py:20
  297.1 2.2 copy.22
  300.8 5.2 copy.21
  306.1 5.2 copy.19
  311.3 2.0 broadcast_select_fusion
  314.3 1.9 broadcast_select_fusion.1
  317.1 2.0 broadcast_select_fusion.13
  320.0 2.1 broadcast_select_fusion.7
  322.1 46.5 %all-gather.2.cloned.1.call-done = f32[32,32,24,128]{3,0,2,1:T(8,128)} async-done(((f32[8,32,24,128]{3,0,2,1:T(8,128)}), f32[32,32,24,128]{3,0,2,1:T(8,128)}) %all-gather.2.cloned.1.call-update) | async-done | bytes 12582928 | tf_op jit(solution)/shard_map/all_gather | solution.py:112
  368.6 12.2 %convolution_bitcast_fusion = f32[1,32,8]{1,2,0:T(8,128)S(1)} fusion(f32[32,32,24,128]{3,0,2,1:T(8,128)} %all-gather.2.cloned.1.call-done, f32[8,32,24,128]{3,0,2,1:T(8,128)S(1)} %copy-done), kind=kOutput, calls=%fused_computation.493 | convolution fusion | flops 301989888 | bytes 15729664 | tf_op jit(solution)/shard_map/dot_general | solution.py:75
  380.9 38.2 %fusion.319 = f32[1,32,8]{1,2,0:T(8,128)S(1)} fusion(f32[32,32,24,128]{3,0,2,1:T(8,128)} %all-gather.2.cloned.1.call-done, f32[8,32,24,128]{3,0,2,1:T(8,128)S(1)} %copy-done, f32[8,6,24,128]{3,0,2,1:T(8,128)} %broadcast_select_fusion.12, f32[8,6,24,128]{3,0,2,1:T(8,128)} %broadcast_select_fusion.13, f32[8,32,6,128]{3,0,2,1:T(8,128)} %broadcast_select_fusion.6, ...), kind=kOutput, calls=%fused_computation.492 | convolution fusion | flops 377487360 | bytes 19170304 | tf_op jit(solution)/shard_map/dot_general | solution.py:78
  419.1 76.8 %psum.7 = f32[2,32,8]{1,2,0:T(8,128)S(1)} all-reduce(f32[2,32,8]{1,2,0:T(8,128)S(1)} %pad_maximum_fusion.21), channel_id=1, replica_groups=mesh['dom'=32,'orb'=4] {'dom'}, use_global_device_ids=true, to_apply=%region_0.1 | all-reduce | flops 512 | bytes 4096 | tf_op jit(solution)/shard_map/psum | solution.py:114
  495.9 20.7 %all_gather.7 = f32[2,32,32]{1,2,0:T(8,128)S(1)} all-gather(f32[2,32,8]{1,2,0:T(8,128)S(1)} %psum.7), channel_id=1, replica_groups=mesh['dom'=32,'orb'=4] {'orb'}, dimensions={2}, use_global_device_ids=true | all-gather | bytes 10240 | tf_op jit(solution)/shard_map/all_gather | solution.py:115
  (55 shorter events, 27.5 us)
Async XLA Ops:
  7.2 361.5 %all-gather.2.cloned.1.call-start = ((), (), s32[]{:S(2)}) async-start(), calls=%async_computation | async-start | bytes 15728640 | tf_op jit(solution)/shard_map/all_gather | solution.py:112
  19.3 28.8 %collective-permute-start.4 = (f32[8,32,24,6]{1,2,3,0:T(8,128)}, f32[8,32,24,6]{1,2,3,0:T(8,128)}, u32[]{:S(2)}, u32[]{:S(2)}) collective-permute-start(f32[8,32,24,6]{1,2,3,0:T(8,128)} %copy.10), channel_id=1, source_target_pairs={{4,0},{8,4},{12,8},{16,12},{20,16},{24,20},{28,24},{32,28},{36,32}... | collective-permute-start | bytes 442376 | tf_op jit(solution)/shard_map/ppermute | solution.py:20
  25.0 22.3 %copy-start.5 = (f32[1,32,24,128]{3,2,1,0:T(8,128)S(1)}, f32[1,32,24,128]{3,2,1,0:T(8,128)}, u32[]{:S(2)}) copy-start(f32[1,32,24,128]{3,2,1,0:T(8,128)} %param.3) | copy-start | bytes 1179652
  25.0 30.0 %collective-permute-start.5 = (f32[8,32,24,6]{1,2,3,0:T(8,128)}, f32[8,32,24,6]{1,2,3,0:T(8,128)}, u32[]{:S(2)}, u32[]{:S(2)}) collective-permute-start(f32[8,32,24,6]{1,2,3,0:T(8,128)} %copy.12), channel_id=1, source_target_pairs={{0,4},{4,8},{8,12},{12,16},{16,20},{20,24},{24,28},{28,32},{32,36}... | collective-permute-start | bytes 442376 | tf_op jit(solution)/shard_map/ppermute | solution.py:20
  31.9 37.2 %collective-permute-start.3 = (f32[8,32,6,128]{3,0,2,1:T(8,128)}, f32[8,32,6,128]{3,0,2,1:T(8,128)}, u32[]{:S(2)}, u32[]{:S(2)}) collective-permute-start(f32[8,32,6,128]{3,0,2,1:T(8,128)} %get-tuple-element.26), channel_id=1, source_target_pairs={{0,8},{4,12},{8,16},{12,20},{16,24},{20,28},{24,32},{28,36},{32,40... | collective-permute-start | bytes 2359304 | tf_op jit(solution)/shard_map/ppermute | solution.py:20
  36.8 42.3 %collective-permute-start.2 = (f32[8,32,6,128]{3,0,2,1:T(8,128)}, f32[8,32,6,128]{3,0,2,1:T(8,128)}, u32[]{:S(2)}, u32[]{:S(2)}) collective-permute-start(f32[8,32,6,128]{3,0,2,1:T(8,128)} %get-tuple-element.25), channel_id=1, source_target_pairs={{8,0},{12,4},{16,8},{20,12},{24,16},{28,20},{32,24},{36,28},{40,32... | collective-permute-start | bytes 2359304 | tf_op jit(solution)/shard_map/ppermute | solution.py:20
  39.2 27.0 %collective-permute-start.1 = (f32[8,6,24,128]{3,0,2,1:T(8,128)}, f32[8,6,24,128]{3,0,2,1:T(8,128)}, u32[]{:S(2)}, u32[]{:S(2)}) collective-permute-start(f32[8,6,24,128]{3,0,2,1:T(8,128)} %get-tuple-element.24), channel_id=1, source_target_pairs={{0,32},{4,36},{8,40},{12,44},{16,48},{20,52},{24,56},{28,60},{32,6... | collective-permute-start | bytes 1769480 | tf_op jit(solution)/shard_map/ppermute | solution.py:20
  48.1 19.0 %collective-permute-start = (f32[8,6,24,128]{3,0,2,1:T(8,128)}, f32[8,6,24,128]{3,0,2,1:T(8,128)}, u32[]{:S(2)}, u32[]{:S(2)}) collective-permute-start(f32[8,6,24,128]{3,0,2,1:T(8,128)} %get-tuple-element.23), channel_id=1, source_target_pairs={{32,0},{36,4},{40,8},{44,12},{48,16},{52,20},{56,24},{60,28},{64,3... | collective-permute-start | bytes 1769480 | tf_op jit(solution)/shard_map/ppermute | solution.py:20
  60.3 4.1 copy-start.3
  115.5 6.7 %copy-start.1 = (f32[8,32,24,128]{3,0,2,1:T(8,128)S(1)}, f32[8,32,24,128]{3,0,2,1:T(8,128)}, u32[]{:S(2)}) copy-start(f32[8,32,24,128]{3,0,2,1:T(8,128)} %get-tuple-element.9) | copy-start | bytes 9437188
  128.0 21.5 %collective-permute-start.11 = (f32[8,32,24,6]{1,2,3,0:T(8,128)}, f32[8,32,24,6]{1,2,3,0:T(8,128)}, u32[]{:S(2)}, u32[]{:S(2)}) collective-permute-start(f32[8,32,24,6]{1,2,3,0:T(8,128)} %copy.16), channel_id=1, source_target_pairs={{0,4},{4,8},{8,12},{12,16},{16,20},{20,24},{24,28},{28,32},{32,36}... | collective-permute-start | bytes 442376 | tf_op jit(solution)/shard_map/ppermute | solution.py:20
  134.5 47.3 %collective-permute-start.10 = (f32[8,32,24,6]{1,2,3,0:T(8,128)}, f32[8,32,24,6]{1,2,3,0:T(8,128)}, u32[]{:S(2)}, u32[]{:S(2)}) collective-permute-start(f32[8,32,24,6]{1,2,3,0:T(8,128)} %copy.14), channel_id=1, source_target_pairs={{4,0},{8,4},{12,8},{16,12},{20,16},{24,20},{28,24},{32,28},{36,32}... | collective-permute-start | bytes 442376 | tf_op jit(solution)/shard_map/ppermute | solution.py:20
  135.8 58.9 %collective-permute-start.9 = (f32[8,32,6,128]{3,0,2,1:T(8,128)}, f32[8,32,6,128]{3,0,2,1:T(8,128)}, u32[]{:S(2)}, u32[]{:S(2)}) collective-permute-start(f32[8,32,6,128]{3,0,2,1:T(8,128)} %get-tuple-element.20), channel_id=1, source_target_pairs={{0,8},{4,12},{8,16},{12,20},{16,24},{20,28},{24,32},{28,36},{32,40... | collective-permute-start | bytes 2359304 | tf_op jit(solution)/shard_map/ppermute | solution.py:20
  145.7 50.1 %collective-permute-start.8 = (f32[8,32,6,128]{3,0,2,1:T(8,128)}, f32[8,32,6,128]{3,0,2,1:T(8,128)}, u32[]{:S(2)}, u32[]{:S(2)}) collective-permute-start(f32[8,32,6,128]{3,0,2,1:T(8,128)} %get-tuple-element.19), channel_id=1, source_target_pairs={{8,0},{12,4},{16,8},{20,12},{24,16},{28,20},{32,24},{36,28},{40,32... | collective-permute-start | bytes 2359304 | tf_op jit(solution)/shard_map/ppermute | solution.py:20
  148.1 43.8 %collective-permute-start.6 = (f32[8,6,24,128]{3,0,2,1:T(8,128)}, f32[8,6,24,128]{3,0,2,1:T(8,128)}, u32[]{:S(2)}, u32[]{:S(2)}) collective-permute-start(f32[8,6,24,128]{3,0,2,1:T(8,128)} %get-tuple-element.21), channel_id=1, source_target_pairs={{32,0},{36,4},{40,8},{44,12},{48,16},{52,20},{56,24},{60,28},{64,3... | collective-permute-start | bytes 1769480 | tf_op jit(solution)/shard_map/ppermute | solution.py:20
  149.4 44.5 %collective-permute-start.7 = (f32[8,6,24,128]{3,0,2,1:T(8,128)}, f32[8,6,24,128]{3,0,2,1:T(8,128)}, u32[]{:S(2)}, u32[]{:S(2)}) collective-permute-start(f32[8,6,24,128]{3,0,2,1:T(8,128)} %get-tuple-element.22), channel_id=1, source_target_pairs={{0,32},{4,36},{8,40},{12,44},{16,48},{20,52},{24,56},{28,60},{32,6... | collective-permute-start | bytes 1769480 | tf_op jit(solution)/shard_map/ppermute | solution.py:20
  187.0 3.0 copy-start.4
  234.1 1.9 copy-start
  244.3 55.0 %collective-permute-start.17 = (f32[8,32,24,6]{1,2,3,0:T(8,128)}, f32[8,32,24,6]{1,2,3,0:T(8,128)}, u32[]{:S(2)}, u32[]{:S(2)}) collective-permute-start(f32[8,32,24,6]{1,2,3,0:T(8,128)} %copy.20), channel_id=1, source_target_pairs={{0,4},{4,8},{8,12},{12,16},{16,20},{20,24},{24,28},{28,32},{32,36}... | collective-permute-start | bytes 442376 | tf_op jit(solution)/shard_map/ppermute | solution.py:20
  259.4 46.7 %collective-permute-start.16 = (f32[8,32,24,6]{1,2,3,0:T(8,128)}, f32[8,32,24,6]{1,2,3,0:T(8,128)}, u32[]{:S(2)}, u32[]{:S(2)}) collective-permute-start(f32[8,32,24,6]{1,2,3,0:T(8,128)} %copy.18), channel_id=1, source_target_pairs={{4,0},{8,4},{12,8},{16,12},{20,16},{24,20},{28,24},{32,28},{36,32}... | collective-permute-start | bytes 442376 | tf_op jit(solution)/shard_map/ppermute | solution.py:20
  262.0 57.1 %collective-permute-start.15 = (f32[8,32,6,128]{3,0,2,1:T(8,128)}, f32[8,32,6,128]{3,0,2,1:T(8,128)}, u32[]{:S(2)}, u32[]{:S(2)}) collective-permute-start(f32[8,32,6,128]{3,0,2,1:T(8,128)} %get-tuple-element.14), channel_id=1, source_target_pairs={{0,8},{4,12},{8,16},{12,20},{16,24},{20,28},{24,32},{28,36},{32,40... | collective-permute-start | bytes 2359304 | tf_op jit(solution)/shard_map/ppermute | solution.py:20
  266.5 53.5 %collective-permute-start.14 = (f32[8,32,6,128]{3,0,2,1:T(8,128)}, f32[8,32,6,128]{3,0,2,1:T(8,128)}, u32[]{:S(2)}, u32[]{:S(2)}) collective-permute-start(f32[8,32,6,128]{3,0,2,1:T(8,128)} %get-tuple-element.13), channel_id=1, source_target_pairs={{8,0},{12,4},{16,8},{20,12},{24,16},{28,20},{32,24},{36,28},{40,32... | collective-permute-start | bytes 2359304 | tf_op jit(solution)/shard_map/ppermute | solution.py:20
  268.9 47.3 %collective-permute-start.13 = (f32[8,6,24,128]{3,0,2,1:T(8,128)}, f32[8,6,24,128]{3,0,2,1:T(8,128)}, u32[]{:S(2)}, u32[]{:S(2)}) collective-permute-start(f32[8,6,24,128]{3,0,2,1:T(8,128)} %get-tuple-element.16), channel_id=1, source_target_pairs={{0,32},{4,36},{8,40},{12,44},{16,48},{20,52},{24,56},{28,60},{32,6... | collective-permute-start | bytes 1769480 | tf_op jit(solution)/shard_map/ppermute | solution.py:20
  299.3 17.7 %collective-permute-start.12 = (f32[8,6,24,128]{3,0,2,1:T(8,128)}, f32[8,6,24,128]{3,0,2,1:T(8,128)}, u32[]{:S(2)}, u32[]{:S(2)}) collective-permute-start(f32[8,6,24,128]{3,0,2,1:T(8,128)} %get-tuple-element.15), channel_id=1, source_target_pairs={{32,0},{36,4},{40,8},{44,12},{48,16},{52,20},{56,24},{60,28},{64,3... | collective-permute-start | bytes 1769480 | tf_op jit(solution)/shard_map/ppermute | solution.py:20
  311.3 3.0 copy-start.2
Sparse Core Ops, SparseCore 0:
  234.3 134.3 all-gather.1
where the time goes:
time: 531 us; the launch traced here: 525 us
  starting transfers between devices  113 us (21%)
  other arithmetic  103 us (19%)
  blocking collectives  97.5 us (18%)
  local copies, waits for them, and re-layouts  90.9 us (17%)
  waiting for transfers between devices  55.9 us (11%)
  matrix products  50.5 us (10%)
  between operations  14.4 us (3%)
    ppermute x18, starting transfers between devices, from_behind(): return lax.ppermute(block, axis, route)  113 us
    psum x1, blocking collectives, shards(): summed_cols = lax.psum(partial_cols, 'dom')  76.8 us
    all_gather x1, waiting for transfers between devices, shards(): piece = lax.all_gather(result, 'orb', axis=0, tiled=True)  46.5 us
    dot_general x1, matrix products, gram_pair(): jnp.dot(left, right_two.T, precision=lax.Precision.HIGHEST, preferred_ele...  38.2 us
    sub x1, other arithmetic, chebyshev(): 2.0 * sigma_next / half_width * (apply_fn(current) - middle * current)  36.2 us
    slice x12, local copies, waits for them, and re-layouts, extend(): lower_face = lax.slice_in_dim(values, 0, HALO, axis=axis_pos)  35 us
    mul x1, other arithmetic, chebyshev(): current = sigma_now / half_width * (apply_fn(start) - middle * start)  34.3 us
    ppermute x6, local copies, waits for them, and re-layouts, from_behind(): return lax.ppermute(block, axis, route)  31.4 us
  transfers between devices with their start and end apart: 19, of which 3 were waited for; matrix products, arithmetic and copies ran while one was open for 17% of the time, Pallas kernels for 0%

commit v1 on v0

v1 whole, which is shorter than its diff:
```python
import math

import jax
import jax.numpy as jnp
import numpy as np
from jax import lax
from jax.experimental import pallas as pl
from jax.experimental.pallas import tpu as pltpu
from jax.sharding import PartitionSpec as P

HALO = 6
SPACING = 0.5
UPPER = 44.0
CUTOFF = 4.0
LOWEST = -1.0
NX, NY, NZ, NO = 32, 24, 128, 8
CELLS = 3145728
CHUNK = 8
ORDER = (0, 3, 1, 2)
MESH = pl.DeviceIdType.MESH
F32, BF16 = jnp.float32, jnp.bfloat16
HIGH = lax.Precision.HIGHEST


def stencil_weights():
    return [
        2.0 * (-1.0) ** (m + 1) * math.factorial(HALO) ** 2
        / (m * m * math.factorial(HALO - m) * math.factorial(HALO + m))
        for m in range(1, HALO + 1)
    ]


WEIGHTS = stencil_weights()
KINETIC = -0.5 / SPACING**2
CENTRE = KINETIC * 3.0 * (-2.0 * sum(WEIGHTS))
HALF = (UPPER - CUTOFF) / 2.0
MIDDLE = (UPPER + CUTOFF) / 2.0
SIGMA1 = HALF / (LOWEST - MIDDLE)
SIGMA2 = 1.0 / (2.0 / SIGMA1 - SIGMA1)


def doubled(matrix):
    wide = matrix.astype(np.float32)
    hi = wide.astype(BF16)
    lo = (wide - hi.astype(np.float32)).astype(BF16)
    row = np.concatenate([hi, lo], axis=1)
    return np.concatenate([row, row], axis=0)


def z_matrices():
    own = np.zeros((NZ, NZ))
    above = np.zeros((NZ, NZ))
    below = np.zeros((NZ, NZ))
    for z in range(NZ):
        for m in range(1, HALO + 1):
            weight = KINETIC * WEIGHTS[m - 1]
            for k in (z - m, z + m):
                if 0 <= k < NZ:
                    own[k, z] = weight
                elif k >= NZ:
                    above[k - NZ, z] = weight
                else:
                    below[k + HALO, z] = weight
    return np.stack([doubled(own), doubled(above), doubled(below)])


def split_wide(v):
    hi = v.astype(BF16)
    lo = (v - hi.astype(F32)).astype(BF16)
    return jnp.concatenate([hi, lo], axis=1)


def split_tall(v):
    hi = v.astype(BF16).astype(F32)
    return jnp.concatenate([hi, v - hi], axis=0).astype(BF16)


def gram(left, right):
    rows, cols = left.shape[0], right.shape[0]
    full = lax.dot_general(
        split_tall(left), split_tall(right), (((1,), (1,)), ((), ())), preferred_element_type=F32
    )
    return (full[:rows, :cols] + full[rows:, :cols]) + (full[:rows, cols:] + full[rows:, cols:])


def flat(block):
    return jnp.concatenate([block[j] for j in range(block.shape[0])], axis=1)


def kernel(orb_hbm, pot_hbm, zmat_ref, out_hbm, cor_ref, sub_ref,
           inp, pot, e0, e1, e2, hf, zacc, potb, zf, zh, oc, oh, gb, part, ar,
           in_sem, pot_sem, out_sem,
           y_ss, y_rs, x_ss, x_rs, z_ss, z_rs, oc_ss, oc_rs, oh_ss, oh_rs, g_ss, g_rs, a_ss, a_rs):
    d = lax.axis_index("dom")
    o = lax.axis_index("orb")
    bx, by, bz = d // 8, (d // 2) % 4, d % 2
    chip, core = o // 2, o % 2
    px, pzl = d % 4, (d // 4) % 2
    other_core = (d, o + 1 - 2 * core)
    other_chip = (d, (o + 2) % 4)
    group = [(d, (o + j) % 4) for j in (1, 2, 3)]
    xs = [((d // 4) * 4 + (px + j) % 4, o) for j in (1, 2, 3)]
    ys = [((d + 8 * j) % 32, o) for j in (1, 2, 3)]
    zl = ((d + 4 - 8 * pzl), o)
    lower = {"x": (d - 8, o), "y": (d - 2, o)}
    upper = {"x": (d + 8, o), "y": (d + 2, o)}
    has_lower = {"x": bx > 0, "y": by > 0}
    has_upper = {"x": bx < 3, "y": by < 3}
    is_a, is_b = chip == 0, chip == 1

    def when(cond, fn):
        if cond is None:
            fn()
        else:
            pl.when(cond)(lambda: fn() and None)

    loads = [
        pltpu.make_async_copy(
            orb_hbm.at[:, 0, pl.ds(CHUNK * k, CHUNK)], inp.at[:, pl.ds(CHUNK * k, CHUNK)], in_sem.at[k])
        for k in range(4)
    ]
    for k in ORDER:
        loads[k].start()
    pot_load = pltpu.make_async_copy(pot_hbm.at[0], pot, pot_sem)
    pot_load.start()

    barrier = pltpu.get_barrier_semaphore()
    for dev in group + xs + ys + [zl]:
        pl.semaphore_signal(barrier, inc=1, device_id=dev, device_id_type=MESH)

    @pl.when(by == 1)
    def _():
        pl.semaphore_signal(barrier, inc=1, device_id=upper["y"], device_id_type=MESH)

    @pl.when(by == 2)
    def _():
        pl.semaphore_signal(barrier, inc=1, device_id=lower["y"], device_id_type=MESH)

    for buf in (e0, e1, e2):
        @pl.when(bx == 0)
        def _(buf=buf):
            buf[0:HALO] = jnp.zeros((HALO, NY + 12, 8, 128), F32)

        @pl.when(bx == 3)
        def _(buf=buf):
            buf[NX + HALO:] = jnp.zeros((HALO, NY + 12, 8, 128), F32)

        @pl.when(by == 0)
        def _(buf=buf):
            @pl.loop(0, NX)
            def _(x):
                buf[HALO + x, 0:HALO] = jnp.zeros((HALO, 8, 128), F32)

        @pl.when(by == 3)
        def _(buf=buf):
            @pl.loop(0, NX)
            def _(x):
                buf[HALO + x, NY + HALO:] = jnp.zeros((HALO, 8, 128), F32)

    pl.semaphore_wait(barrier, 10 + jnp.where((by == 1) | (by == 2), 1, 0))

    def y_copy(stage, buf, k, side):
        rows = pl.ds(HALO + CHUNK * k, CHUNK)
        src, dst = ((HALO, NY + HALO), (NY, 0))[side]
        return pltpu.make_async_remote_copy(
            src_ref=buf.at[rows, pl.ds(src, HALO)], dst_ref=buf.at[rows, pl.ds(dst, HALO)],
            send_sem=y_ss.at[stage, k, side], recv_sem=y_rs.at[stage, k, side],
            device_id=(lower, upper)[side]["y"], device_id_type=MESH)

    def x_copy(stage, buf, side):
        src, dst = ((HALO, NX + HALO), (NX, 0))[side]
        cols = pl.ds(HALO, NY)
        return pltpu.make_async_remote_copy(
            src_ref=buf.at[pl.ds(src, HALO), cols], dst_ref=buf.at[pl.ds(dst, HALO), cols],
            send_sem=x_ss.at[stage, side], recv_sem=x_rs.at[stage, side],
            device_id=(lower, upper)[side]["x"], device_id_type=MESH)

    def z_copy(stage):
        return pltpu.make_async_remote_copy(
            src_ref=zf.at[stage], dst_ref=zh.at[stage],
            send_sem=z_ss.at[stage], recv_sem=z_rs.at[stage],
            device_id=(d + 1 - 2 * bz, o), device_id_type=MESH)

    def sends(axis, side):
        return (has_lower, has_upper)[side][axis]

    def receives(axis, side):
        return (has_upper, has_lower)[side][axis]

    def send_y(stage, buf, k):
        for side in (0, 1):
            when(sends("y", side), lambda: y_copy(stage, buf, k, side).start())

    def wait_y(stage, buf, k):
        for side in (0, 1):
            when(receives("y", side), lambda: y_copy(stage, buf, k, side).wait_recv())

    def send_x(stage, buf, side):
        when(sends("x", side), lambda: x_copy(stage, buf, side).start())

    def wait_x(stage, buf):
        for side in (0, 1):
            when(receives("x", side), lambda: x_copy(stage, buf, side).wait_recv())

    lane = lax.broadcasted_iota(jnp.int32, (8, 128), 1)

    def pack_z(stage, buf):
        first = jnp.where(bz == 0, NZ - HALO, 0)

        @pl.loop(0, 2)
        def _(half):
            @pl.loop(0, NY)
            def _(y):
                total = None
                for x in range(16):
                    moved = pltpu.roll(
                        buf[HALO + 16 * half + x, HALO + y], lax.rem(8 * x + 128 - first, 128), axis=1)
                    total = moved if total is None else jnp.where(lane // 8 == x, moved, total)
                zf[stage, half, y] = total

    def z_own(buf):
        @pl.loop(0, NX // 4)
        def _(t):
            v = buf[pl.ds(HALO + 4 * t, 4), pl.ds(HALO, NY)].reshape(4 * NY * 8, 128)
            r = jnp.dot(split_wide(v), zmat_ref[0], preferred_element_type=F32)
            zacc[pl.ds(4 * t, 4)] = (r[:, :128] + r[:, 128:]).reshape(4, NY, 8, 128)

    def z_halo(stage):
        @pl.loop(0, NX // 4)
        def _(t):
            parts = []
            for j in range(4):
                x = 4 * t + j
                packed = zh[stage, x // 16].reshape(NY * 8, 128)
                parts.append(pltpu.roll(packed, lax.rem(128 - 8 * lax.rem(x, 16), 128), axis=1))
            v = jnp.concatenate(parts, axis=0)
            r = jnp.dot(split_wide(v), zmat_ref[1 + bz], preferred_element_type=F32)
            zacc[pl.ds(4 * t, 4)] += (r[:, :128] + r[:, 128:]).reshape(4, NY, 8, 128)

    def rows_of(src, dst, off, x, y, scale, shift, prev, prev_scale):
        def at(dx, dy):
            return src[x + HALO + dx, pl.ds(y + HALO + dy, HALO)]

        total = scale * zacc[x, pl.ds(y, HALO)]
        total += (scale * potb[x, pl.ds(y, HALO)] + (scale * CENTRE + shift)) * at(0, 0)
        for m in range(1, HALO + 1):
            near = (at(m, 0) + at(-m, 0)) + (at(0, m) + at(0, -m))
            total += (scale * KINETIC * WEIGHTS[m - 1]) * near
        if prev is not None:
            total -= prev_scale * prev[x + HALO, pl.ds(y + HALO, HALO)]
        dst[x + off, pl.ds(y + off, HALO)] = total

    def stage_rows(lo, hi, ys_, *args):
        @pl.loop(lo, hi)
        def _(x):
            for y in ys_:
                rows_of(args[0], args[1], args[2], x, y, *args[3:])

    pend = []

    def stage(n, src, dst, off, scale, shift, prev, prev_scale, after):
        args = (src, dst, off, scale, shift, prev, prev_scale)
        z_own(src)
        z_copy(n).wait_recv()
        z_halo(n)
        stage_rows(HALO, NX - HALO, (6, 12), *args)
        wait_x(n, src)
        stage_rows(0, HALO, (6, 12), *args)
        stage_rows(NX - HALO, NX, (6, 12), *args)
        for k in ORDER:
            wait_y(n, src, k)
            stage_rows(CHUNK * k, CHUNK * k + CHUNK, (0, 18), *args)
            after(k)

    def pass_on(n, buf, k):
        send_y(n, buf, k)
        if k == 0:
            send_x(n, buf, 0)
        if k == 3:
            send_x(n, buf, 1)

    flat_in = inp.reshape(NO * NX * NY, 128)
    for k in ORDER:
        loads[k].wait()

        @pl.loop(CHUNK * k, CHUNK * k + CHUNK)
        def _(x):
            for y in range(NY):
                e0[HALO + x, HALO + y] = flat_in[pl.ds(x * NY + y, 8, stride=NX * NY), :]
        pass_on(0, e0, k)
    pack_z(0, e0)
    z_copy(0).start()
    pot_load.wait()

    @pl.loop(0, NX)
    def _(x):
        for y in range(NY):
            potb[x, y] = jnp.broadcast_to(pot[x, pl.ds(y, 1)], (8, 128))

    stage(0, e0, e1, HALO, SIGMA1 / HALF, -SIGMA1 / HALF * MIDDLE, None, 0.0,
          lambda k: pass_on(1, e1, k))
    pack_z(1, e1)
    z_copy(1).start()

    def core_copy(k):
        return pltpu.make_async_remote_copy(
            src_ref=e2.at[pl.ds(HALO + CHUNK * k, CHUNK), pl.ds(HALO, NY)],
            dst_ref=oc.at[pl.ds(CHUNK * k, CHUNK)],
            send_sem=oc_ss.at[k], recv_sem=oc_rs.at[k], device_id=other_core, device_id_type=MESH)

    def chip_copy(src, y, slot, k):
        return pltpu.make_async_remote_copy(
            src_ref=src, dst_ref=gb.at[slot, pl.ds(CHUNK * k, CHUNK)],
            send_sem=g_ss.at[slot, k], recv_sem=g_rs.at[slot, k],
            device_id=other_chip, device_id_type=MESH)

    def f_rows(k, y):
        return e2.at[pl.ds(HALO + CHUNK * k, CHUNK), pl.ds(HALO + y, 8)]

    def f_copies(k):
        pass_on(2, e2, k)
        core_copy(k).start()

        @pl.when(is_a)
        def _():
            chip_copy(f_rows(k, 0), 0, 0, k).start()
            chip_copy(f_rows(k, 16), 16, 1, k).start()

        @pl.when(is_b)
        def _():
            chip_copy(f_rows(k, 8), 8, 0, k).start()

    s2 = 2.0 * SIGMA2 / HALF
    stage(1, e1, e2, HALO, s2, -s2 * MIDDLE, e0, SIGMA1 * SIGMA2, f_copies)
    pack_z(2, e2)
    z_copy(2).start()

    @pl.loop(0, NX)
    def _(x):
        for orb in range(NO):
            inp[orb, x] = e2[HALO + x, pl.ds(HALO, NY), orb]
    out_copy = pltpu.make_async_copy(inp, out_hbm.at[:, 0], out_sem)
    out_copy.start()

    def h_rows(k, y):
        return hf.at[pl.ds(CHUNK * k, CHUNK), pl.ds(y, 8)]

    def oh_copy(k, j):
        return pltpu.make_async_remote_copy(
            src_ref=h_rows(k, 16 * j), dst_ref=oh.at[pl.ds(CHUNK * k, CHUNK), pl.ds(8 * j, 8)],
            send_sem=oh_ss.at[k, j], recv_sem=oh_rs.at[k, j], device_id=other_core, device_id_type=MESH)

    def h_copies(k):
        @pl.when(is_b)
        def _():
            chip_copy(h_rows(k, 8), 8, 1, k).start()
            for j in (0, 1):
                oh_copy(k, j).start()

    stage(2, e2, hf, 0, 1.0, 0.0, None, 0.0, h_copies)

    part[...] = jnp.zeros_like(part)
    for k in range(4):
        core_copy(k).wait_recv()

    def own_f(x, y, n):
        return flat(e2[HALO + x, pl.ds(HALO + y, n)])

    def in_chip(x, total):
        left = jnp.concatenate([own_f(x, 0, NY), flat(oc[x])], axis=0)
        right = jnp.concatenate([own_f(x, 0, NY), flat(hf[x])], axis=0)
        return total + gram(left, right)

    def place(block, starts):
        n = block.shape[1]
        r = lax.broadcasted_iota(jnp.int32, (n, 128), 0)
        c = lax.broadcasted_iota(jnp.int32, (n, 128), 1)
        chosen = jnp.zeros((n, 128), jnp.bool_)
        for j, s in enumerate(starts):
            chosen = chosen | ((r // 8 == j) & (c == s + r % 8))
        return jnp.dot(block, chosen.astype(F32), precision=HIGH, preferred_element_type=F32)

    def add_rows(orbital, block):
        rows = pl.ds(pl.multiple_of(8 * orbital, 8), 8)
        part[rows, :] += block

    o_core = o + 1 - 2 * core
    o_chip = (o + 2) % 4
    local = lax.fori_loop(0, NX, in_chip, jnp.zeros((16, 16), F32))
    placed = place(local, (8 * o, 32 + 8 * o))
    add_rows(o, placed[:8])
    add_rows(o_core, placed[8:])

    @pl.when(is_a)
    def _():
        for slot in (0, 1):
            for k in range(4):
                chip_copy(f_rows(k, 8), 8, slot, k).wait_recv()

        def cross(x, total):
            left = jnp.concatenate([own_f(x, 8, 8), flat(oc[x, pl.ds(8, 8)])], axis=0)
            right = jnp.concatenate([flat(gb[0, x]), flat(gb[1, x])], axis=0)
            return total + gram(left, right)

        block = place(lax.fori_loop(0, NX, cross, jnp.zeros((16, 16), F32)), (8 * o_chip, 32 + 8 * o_chip))
        add_rows(o, block[:8])
        add_rows(o_core, block[8:])

    @pl.when(is_b)
    def _():
        for slot in (0, 1):
            for k in range(4):
                chip_copy(f_rows(k, 8), 8, slot, k).wait_recv()
        for k in range(4):
            for j in (0, 1):
                oh_copy(k, j).wait_recv()

        def cross(x, total):
            left = jnp.concatenate([flat(gb[0, x]), flat(gb[1, x])], axis=1)
            right = [
                jnp.concatenate([own_f(x, 0, 8), own_f(x, 16, 8)], axis=1),
                jnp.concatenate([flat(oc[x, pl.ds(0, 8)]), flat(oc[x, pl.ds(16, 8)])], axis=1),
                jnp.concatenate([flat(hf[x, pl.ds(0, 8)]), flat(hf[x, pl.ds(16, 8)])], axis=1),
                flat(oh[x]),
            ]
            return total + gram(left, jnp.concatenate(right, axis=0))

        block = place(lax.fori_loop(0, NX, cross, jnp.zeros((8, 32), F32)),
                      (8 * o, 8 * o_core, 32 + 8 * o, 32 + 8 * o_core))
        add_rows(o_chip, block)

    def reduce(step, mine, count, partners):
        ar[step, mine] = part[...]
        copies = []
        for j, dev in enumerate(partners):
            copies.append(pltpu.make_async_remote_copy(
                src_ref=ar.at[step, mine], dst_ref=ar.at[step, mine],
                send_sem=a_ss.at[step, j], recv_sem=a_rs.at[step, mine],
                device_id=dev, device_id_type=MESH))
            copies[-1].start()
        for j, dev in enumerate(partners):
            source = lax.rem(mine + j + 1, count)
            pltpu.make_async_remote_copy(
                src_ref=ar.at[step, source], dst_ref=ar.at[step, source],
                send_sem=a_ss.at[step, j], recv_sem=a_rs.at[step, source],
                device_id=dev, device_id_type=MESH).wait_recv()
        total = ar[step, 0]
        for j in range(1, count):
            total += ar[step, j]
        part[...] = total
        for c in copies:
            c.wait_send()

    reduce(0, o, 4, group)
    reduce(1, px, 4, xs)
    reduce(2, bx, 4, ys)
    reduce(3, pzl, 2, [zl])

    square = part[...]
    r = lax.broadcasted_iota(jnp.int32, (32, 32), 0)
    c = lax.broadcasted_iota(jnp.int32, (32, 32), 1)
    eye = (r == c).astype(F32)
    for at, ref, factor in ((0, cor_ref, 1.0 / CELLS), (32, sub_ref, 1.0 / (CELLS * HALF))):
        m = square[:, at:at + 32]
        t = lax.dot_general(m, eye, (((0,), (0,)), ((), ())), precision=HIGH, preferred_element_type=F32)
        ref[...] = jnp.where((r >= 16) & (c < 16), t, m) * factor

    out_copy.wait()
    for n, buf in ((0, e0), (1, e1), (2, e2)):
        for side in (0, 1):
            for k in range(4):
                when(sends("y", side), lambda: y_copy(n, buf, k, side).wait_send())
            when(sends("x", side), lambda: x_copy(n, buf, side).wait_send())
        z_copy(n).wait_send()
    for k in range(4):
        core_copy(k).wait_send()
        for slot in (0, 1):
            chip_copy(f_rows(k, 8), 8, slot, k).wait_send()

    @pl.when(is_b)
    def _():
        for k in range(4):
            for j in (0, 1):
                oh_copy(k, j).wait_send()


def shards(orbitals, potential):
    zmat = jnp.asarray(z_matrices())
    field = (NX + 12, NY + 12, 8, 128)
    vm = lambda *shape: pltpu.VMEM(shape, F32)
    dma = lambda *shape: pltpu.SemaphoreType.DMA(shape)
    out, cor, sub = pl.pallas_call(
        kernel,
        out_shape=(
            jax.ShapeDtypeStruct((NO, 1, NX, NY, NZ), F32),
            jax.ShapeDtypeStruct((32, 32), F32),
            jax.ShapeDtypeStruct((32, 32), F32),
        ),
        in_specs=[pl.BlockSpec(memory_space=pl.ANY)] * 2 + [pl.BlockSpec(memory_space=pltpu.VMEM)],
        out_specs=(pl.BlockSpec(memory_space=pl.ANY),) + (pl.BlockSpec(memory_space=pltpu.VMEM),) * 2,
        scratch_shapes=[
            vm(NO, NX, NY, NZ), vm(NX, NY, NZ), vm(*field), vm(*field), vm(*field),
            vm(NX, NY, 8, 128), vm(NX, NY, 8, 128), vm(NX, NY, 8, 128),
            vm(3, 2, NY, 8, 128), vm(3, 2, NY, 8, 128),
            vm(NX, NY, 8, 128), vm(NX, 16, 8, 128), vm(2, NX, 8, 8, 128),
            vm(32, 128), vm(4, 4, 32, 128),
            dma(4), pltpu.SemaphoreType.DMA, pltpu.SemaphoreType.DMA,
            dma(3, 4, 2), dma(3, 4, 2), dma(3, 2), dma(3, 2), dma(3), dma(3),
            dma(4), dma(4), dma(4, 2), dma(4, 2), dma(2, 4), dma(2, 4), dma(4, 3), dma(4, 4),
        ],
        compiler_params=pltpu.CompilerParams(
            collective_id=0, has_side_effects=True, vmem_limit_bytes=58 * 2**20),
        name="filter_and_subspace",
    )(orbitals, potential, zmat)
    return out, cor, sub


def solution(mesh):
    placed = (P("orb", "dom", None, None, None), P("dom", None, None, None))
    return jax.shard_map(
        shards,
        mesh=mesh,
        in_specs=placed,
        out_specs=(P("orb", "dom", None, None, None), P(), P()),
        check_vma=False,
    )
```

time: 531 us -> 190 us (0.36)
  Pallas kernels: 0 us -> 182 us
  starting transfers between devices: 113 us -> 0 us
  other arithmetic: 103 us -> 0 us
  blocking collectives: 97.5 us -> 0 us
  local copies, waits for them, and re-layouts: 90.9 us -> 5.01 us
  waiting for transfers between devices: 55.9 us -> 0 us
  matrix products: 50.5 us -> 0 us
  between operations: 14.4 us -> 0.66 us
    pallas_call x0 -> x1, Pallas kernels: none -> 182 us  [shards(): pl.pallas_call(kernel, out_shape=(jax.ShapeDtypeStruct((NO, 1, NX, NY, NZ...]
    ppermute x18 -> x0, starting transfers between devices: 113 us -> none  [from_behind(): return lax.ppermute(block, axis, route)]
    psum x1 -> x0, blocking collectives: 76.8 us -> none  [shards(): summed_cols = lax.psum(partial_cols, 'dom')]
    dot_general x2 -> x0, matrix products: 50.5 us -> none  [the longest x1 38.2 us: gram_pair(): jnp.dot(left, right_two.T, precision=lax.Precision.HIGHEST, preferred_ele...]
    slice x15 -> x0, local copies, waits for them, and re-layouts: 48.4 us -> none  [the longest x12 35 us: extend(): lower_face = lax.slice_in_dim(values, 0, HALO, axis=axis_pos)]
    all_gather x1 -> x0, waiting for transfers between devices: 46.5 us -> none  [shards(): piece = lax.all_gather(result, 'orb', axis=0, tiled=True)]
    sub x1 -> x0, other arithmetic: 36.2 us -> none  [chebyshev(): 2.0 * sigma_next / half_width * (apply_fn(current) - middle * current)]
    mul x2 -> x0, other arithmetic: 35.1 us -> none  [the longest x1 34.3 us: chebyshev(): current = sigma_now / half_width * (apply_fn(start) - middle * start)]
  transfers between devices with their start and end apart: 19 -> 0, of which waited for: 3 -> 0; matrix products, arithmetic and copies ran while one was open for 17% -> 0% of each run, Pallas kernels for 0% -> 0%
where the time goes in v1:
time: 190 us; the launch traced here: 188 us
  Pallas kernels  182 us (96%)
  local copies, waits for them, and re-layouts  5.01 us (3%)
    pallas_call x1, Pallas kernels, shards(): pl.pallas_call(kernel, out_shape=(jax.ShapeDtypeStruct((NO, 1, NX, NY, NZ...  182 us
    unnamed x7, local copies, waits for them, and re-layouts  5.01 us

profile of v1, /device:TPU:1, one launch (start us, length us, event | category | flops | bytes accessed | tf_op | source)
XLA Modules:
  0.0 188.1 jit_solution(3788485535095012690)
XLA Ops:
  0.6 182.4 %filter_and_subspace.1 = (f32[8,1,32,24,128]{4,3,2,1,0:T(8,128)}, f32[32,32]{1,0:T(8,128)}, f32[32,32]{1,0:T(8,128)}) custom-call(f32[8,1,32,24,128]{4,3,2,1,0:T(8,128)} %orb_hbm.1, f32[1,32,24,128]{3,2,1,0:T(8,128)} %pot_hbm.1, bf16[3,256,256]{2,1,0:T(8,128)(2,1)} %constant.2.clone.zmat_ref), custom_call_target="tpu_custom_call" | custom-call | tf_op jit(solution)/shard_map/filter_and_subspace/pallas_call | solution.py:492
  183.0 0.0 copy-start.1
  183.0 0.0 copy-start
  183.1 3.8 %copy.9 = f32[8,1,32,24,128]{4,3,2,1,0:T(8,128)} copy(f32[8,1,32,24,128]{4,3,2,1,0:T(8,128)} %get-tuple-element.6) | data formatting | bytes 6291456
  186.8 0.0 copy-done.1
  186.9 0.6 copy.10
  187.5 0.0 copy-done
  187.5 0.6 copy.11
Async XLA Ops:
  183.0 3.8 %copy-start.1 = (f32[32,32]{1,0:T(8,128)S(1)}, f32[32,32]{1,0:T(8,128)}, u32[]{:S(2)}) copy-start(f32[32,32]{1,0:T(8,128)} %get-tuple-element.7) | copy-start | bytes 12292
  183.0 4.4 %copy-start = (f32[32,32]{1,0:T(8,128)S(1)}, f32[32,32]{1,0:T(8,128)}, u32[]{:S(2)}) copy-start(f32[32,32]{1,0:T(8,128)} %get-tuple-element.8) | copy-start | bytes 12292

commit v2 on v1

v2 whole, which is shorter than its diff:
```python
import math

import jax
import jax.numpy as jnp
import numpy as np
from jax import lax
from jax.experimental import pallas as pl
from jax.experimental.pallas import tpu as pltpu
from jax.sharding import PartitionSpec as P

HALO = 6
SPACING = 0.5
UPPER = 44.0
CUTOFF = 4.0
LOWEST = -1.0
NX, NY, NZ, NO = 32, 24, 128, 8
CELLS = 3145728
CHUNK = 4
ORDERS = ((0, 1, 7, 6, 4, 5, 2, 3), (0, 4, 1, 5, 2, 6, 3, 7))
FLIGHT = 3
ROWS = ((6, 12), (0, 6), (18, 6))
MESH = pl.DeviceIdType.MESH
F32, BF16 = jnp.float32, jnp.bfloat16
HIGH = lax.Precision.HIGHEST


def stencil_weights():
    return [
        2.0 * (-1.0) ** (m + 1) * math.factorial(HALO) ** 2
        / (m * m * math.factorial(HALO - m) * math.factorial(HALO + m))
        for m in range(1, HALO + 1)
    ]


WEIGHTS = stencil_weights()
KINETIC = -0.5 / SPACING**2
CENTRE = KINETIC * 3.0 * (-2.0 * sum(WEIGHTS))
HALF = (UPPER - CUTOFF) / 2.0
MIDDLE = (UPPER + CUTOFF) / 2.0
SIGMA1 = HALF / (LOWEST - MIDDLE)
SIGMA2 = 1.0 / (2.0 / SIGMA1 - SIGMA1)


def doubled(matrix):
    wide = matrix.astype(np.float32)
    hi = wide.astype(BF16)
    lo = (wide - hi.astype(np.float32)).astype(BF16)
    row = np.concatenate([hi, lo], axis=1)
    return np.concatenate([row, row], axis=0)


def z_matrices():
    own = np.zeros((NZ, NZ))
    above = np.zeros((NZ, NZ))
    below = np.zeros((NZ, NZ))
    for z in range(NZ):
        for m in range(1, HALO + 1):
            weight = KINETIC * WEIGHTS[m - 1]
            for k in (z - m, z + m):
                if 0 <= k < NZ:
                    own[k, z] = weight
                elif k >= NZ:
                    above[k - NZ, z] = weight
                else:
                    below[k + HALO, z] = weight
    upper = np.zeros((NZ, NZ))
    top = np.zeros((NZ, NZ))
    for z in range(NZ):
        g, at = z // 64, z % 64
        for m in range(1, HALO + 1):
            weight = KINETIC * WEIGHTS[m - 1]
            if at + m < 64:
                upper[z + m, z] = weight
            else:
                top[8 * g + at + m - 64, z] = weight
    return np.stack([doubled(v) for v in (own, above, below, upper, top)])


def split_wide(v):
    hi = v.astype(BF16)
    lo = (v - hi.astype(F32)).astype(BF16)
    return jnp.concatenate([hi, lo], axis=1)


def split_tall(v):
    hi = v.astype(BF16).astype(F32)
    return jnp.concatenate([hi, v - hi], axis=0).astype(BF16)


def gram(left, right):
    rows, cols = left.shape[0], right.shape[0]
    full = lax.dot_general(
        split_tall(left), split_tall(right), (((1,), (1,)), ((), ())), preferred_element_type=F32
    )
    return (full[:rows, :cols] + full[rows:, :cols]) + (full[:rows, cols:] + full[rows:, cols:])


def flat(block):
    return jnp.concatenate([block[j] for j in range(block.shape[0])], axis=1)


def kernel(orb_hbm, pot_hbm, zmat_ref, out_hbm, cor_ref, sub_ref,
           inp, pot, e0, e1, e2, zacc, potb, zf, zh, pf, sb, ocp, hp, tx, potp, zs, zp, part, ar1, ar2,
           in_sem, pot_sem, out_sem,
           y_ss, y_rs, x_ss, x_rs, z_ss, z_rs, c_ss, c_rs, g_ss, g_rs,
           ty_ss, ty_rs, tx_ss, tx_rs, zp_ss, zp_rs, a1_ss, a1_rs, a2_ss, a2_rs):
    d = lax.axis_index("dom")
    o = lax.axis_index("orb")
    bx, by, bz = d // 8, (d // 2) % 4, d % 2
    chip, core = o // 2, o % 2
    px, pzl = d % 4, (d // 4) % 2
    other_core = (d, o + 1 - 2 * core)
    other_chip = (d, (o + 2) % 4)
    column = lambda i: ((d + 4 * (i // 4)) % 8 + 8 * bx, (o + i) % 4)
    plane = lambda i: (((bx + i // 4) % 4) * 8 + 4 * pzl + (px + i) % 4, o)
    columns = [column(i) for i in range(1, 8)]
    planes = [plane(i) for i in range(1, 16)]
    crossed = (d + 1 - 2 * bz, (o + 2) % 4)
    lower = {"x": (d - 8, o), "y": (d - 2, o)}
    upper = {"x": (d + 8, o), "y": (d + 2, o)}
    has_lower = {"x": bx > 0, "y": by > 0}
    has_upper = {"x": bx < 3, "y": by < 3}
    is_a, is_b = chip == 0, chip == 1

    def when(cond, fn):
        if cond is None:
            fn()
        else:
            pl.when(cond)(lambda: fn() and None)

    loads = [
        pltpu.make_async_copy(
            orb_hbm.at[:, 0, pl.ds(8 * k, 8)], inp.at[:, pl.ds(8 * k, 8)], in_sem.at[k])
        for k in range(4)
    ]
    for k in (0, 3, 1, 2):
        loads[k].start()
    pot_load = pltpu.make_async_copy(pot_hbm.at[0], pot, pot_sem)
    pot_load.start()

    barrier = pltpu.get_barrier_semaphore()
    for dev in columns + planes:
        pl.semaphore_signal(barrier, inc=1, device_id=dev, device_id_type=MESH)

    @pl.when(by == 1)
    def _():
        pl.semaphore_signal(barrier, inc=1, device_id=upper["y"], device_id_type=MESH)

    @pl.when(by == 2)
    def _():
        pl.semaphore_signal(barrier, inc=1, device_id=lower["y"], device_id_type=MESH)

    crosses = (is_a & (bz == 1)) | (is_b & (bz == 0))

    @pl.when(crosses)
    def _():
        pl.semaphore_signal(barrier, inc=1, device_id=crossed, device_id_type=MESH)

    for buf in (e0, e1):
        @pl.when(bx == 0)
        def _(buf=buf):
            buf[0:HALO] = jnp.zeros((HALO, NY + 12, 8, 128), F32)

        @pl.when(bx == 3)
        def _(buf=buf):
            buf[NX + HALO:] = jnp.zeros((HALO, NY + 12, 8, 128), F32)

        @pl.when(by == 0)
        def _(buf=buf):
            @pl.loop(0, NX)
            def _(x):
                buf[HALO + x, 0:HALO] = jnp.zeros((HALO, 8, 128), F32)

        @pl.when(by == 3)
        def _(buf=buf):
            @pl.loop(0, NX)
            def _(x):
                buf[HALO + x, NY + HALO:] = jnp.zeros((HALO, 8, 128), F32)

    @pl.when(bx == 3)
    def _():
        tx[...] = jnp.zeros_like(tx)

    @pl.when(by == 3)
    def _():
        @pl.loop(0, 16)
        def _(x):
            for s in (0, 1):
                pf[s, x, NY:] = jnp.zeros((HALO, 8, 128), F32)

    @pl.when(is_b & (bz == 1))
    def _():
        zp[...] = jnp.zeros_like(zp)

    pl.semaphore_wait(barrier, 22 + jnp.where((by == 1) | (by == 2), 1, 0) + jnp.where(crosses, 1, 0))

    def y_copy(stage, buf, k, side):
        rows = pl.ds(HALO + CHUNK * k, CHUNK)
        src, dst = ((HALO, NY + HALO), (NY, 0))[side]
        return pltpu.make_async_remote_copy(
            src_ref=buf.at[rows, pl.ds(src, HALO)], dst_ref=buf.at[rows, pl.ds(dst, HALO)],
            send_sem=y_ss.at[stage, k, side], recv_sem=y_rs.at[stage, k, side],
            device_id=(lower, upper)[side]["y"], device_id_type=MESH)

    def x_copy(stage, buf, side):
        src, dst = ((HALO, NX + HALO), (NX, 0))[side]
        cols = pl.ds(HALO, NY)
        return pltpu.make_async_remote_copy(
            src_ref=buf.at[pl.ds(src, HALO), cols], dst_ref=buf.at[pl.ds(dst, HALO), cols],
            send_sem=x_ss.at[stage, side], recv_sem=x_rs.at[stage, side],
            device_id=(lower, upper)[side]["x"], device_id_type=MESH)

    def z_copies(stage, part):
        return [
            pltpu.make_async_remote_copy(
                src_ref=zf.at[stage, :, pl.ds(*ROWS[r])], dst_ref=zh.at[stage, :, pl.ds(*ROWS[r])],
                send_sem=z_ss.at[stage, r], recv_sem=z_rs.at[stage, r],
                device_id=(d + 1 - 2 * bz, o), device_id_type=MESH)
            for r in ((0,), (1, 2))[part]
        ]

    def sends(axis, side):
        return (has_lower, has_upper)[side][axis]

    def receives(axis, side):
        return (has_upper, has_lower)[side][axis]

    queue = [(n, buf, k) for n, buf in ((0, e0), (1, e1)) for k in ORDERS[n]]
    sent = []

    def pump(last):
        while len(sent) <= min(last, len(queue) - 1):
            q = len(sent)
            if q >= FLIGHT:
                for side in (0, 1):
                    when(sends("y", side), lambda: y_copy(*queue[q - FLIGHT], side).wait_send())
            for side in (0, 1):
                when(sends("y", side), lambda: y_copy(*queue[q], side).start())
            sent.append(q)

    def wait_y(q):
        for side in (0, 1):
            when(receives("y", side), lambda: y_copy(*queue[q], side).wait_recv())

    def send_x(stage, buf, side):
        when(sends("x", side), lambda: x_copy(stage, buf, side).start())

    def wait_x(stage, buf):
        for side in (0, 1):
            when(receives("x", side), lambda: x_copy(stage, buf, side).wait_recv())

    lane = lax.broadcasted_iota(jnp.int32, (8, 128), 1)

    def pack_z(stage, buf, part):
        first = jnp.where(bz == 0, NZ - HALO, 0)
        shifts = [lax.rem(8 * x + 128 - first, 128) for x in range(16)]

        def rows(half, y, n):
            for j in range(n):
                total = None
                for x in range(16):
                    moved = pltpu.roll(buf[HALO + 16 * half + x, HALO + y + j], shifts[x], axis=1)
                    total = moved if total is None else jnp.where(lane // 8 == x, moved, total)
                zf[stage, half, y + j] = total

        @pl.loop(0, 4)
        def _(t):
            if part == 0:
                rows(t // 2, 6 + 6 * (t % 2), 6)
            else:
                rows(t // 2, 18 * (t % 2), 6)
        for copy in z_copies(stage, part):
            copy.start()

    def pack_top(first, dst, slot):
        @pl.loop(0, 2)
        def _(half):
            @pl.loop(0, NY // 4)
            def _(t):
                for j in range(4):
                    total = None
                    for i in range(16):
                        moved = pltpu.roll(
                            e2[HALO + 8 * half + i // 2 + 16 * (i % 2), HALO + 4 * t + j],
                            (8 * i + 128 - first) % 128, axis=1)
                        total = moved if total is None else jnp.where(lane // 8 == i, moved, total)
                    dst[slot, half, 4 * t + j] = total

    def z_own(buf):
        @pl.loop(0, NX // 4)
        def _(t):
            v = buf[pl.ds(HALO + 4 * t, 4), pl.ds(HALO, NY)].reshape(4 * NY * 8, 128)
            r = jnp.dot(split_wide(v), zmat_ref[0], preferred_element_type=F32)
            zacc[pl.ds(4 * t, 4)] = (r[:, :128] + r[:, 128:]).reshape(4, NY, 8, 128)

    def z_halo(stage, part):
        for copy in z_copies(stage, part):
            copy.wait_recv()

        @pl.loop(0, NX // 4)
        def _(t):
            parts = []
            for j in range(4):
                x = 4 * t + j
                packed = [zh[stage, x // 16, pl.ds(*ROWS[r])].reshape(ROWS[r][1] * 8, 128)
                          for r in ((0,), (1, 2))[part]]
                packed = jnp.concatenate(packed, axis=0) if part else packed[0]
                parts.append(pltpu.roll(packed, lax.rem(128 - 8 * lax.rem(x, 16), 128), axis=1))
            v = jnp.concatenate(parts, axis=0)
            r = jnp.dot(split_wide(v), zmat_ref[1 + bz], preferred_element_type=F32)
            r = (r[:, :128] + r[:, 128:]).reshape(4, 12, 8, 128)
            at = pl.ds(4 * t, 4)
            if part == 0:
                zacc[at, pl.ds(6, 12)] += r
            else:
                zacc[at, pl.ds(0, 6)] += r[:, :6]
                zacc[at, pl.ds(18, 6)] += r[:, 6:]

    def rows_of(src, dst, x, y, scale, shift, prev, prev_scale):
        def at(dx, dy):
            return src[x + HALO + dx, pl.ds(y + HALO + dy, HALO)]

        total = scale * zacc[x, pl.ds(y, HALO)]
        total += (scale * potb[x, pl.ds(y, HALO)] + (scale * CENTRE + shift)) * at(0, 0)
        for m in range(1, HALO + 1):
            near = (at(m, 0) + at(-m, 0)) + (at(0, m) + at(0, -m))
            total += (scale * KINETIC * WEIGHTS[m - 1]) * near
        if prev is not None:
            total -= prev_scale * prev[x + HALO, pl.ds(y + HALO, HALO)]
        dst[x + HALO, pl.ds(y + HALO, HALO)] = total

    def stage_rows(lo, hi, ys_, *args):
        @pl.loop(lo, hi)
        def _(x):
            for y in ys_:
                rows_of(args[0], args[1], x, y, *args[2:])

    def interior(n, src, *args):
        z_own(src)
        pump(8 * n + 4 - n)
        z_halo(n, 0)
        stage_rows(HALO, NX - HALO, (6, 12), src, *args)
        pump(8 * n + 5 - 2 * n)
        wait_x(n, src)
        stage_rows(0, HALO, (6, 12), src, *args)
        stage_rows(NX - HALO, NX, (6, 12), src, *args)

    def faces(n, *args):
        for j, k in enumerate(ORDERS[n]):
            wait_y(8 * n + j)
            stage_rows(CHUNK * k, CHUNK * k + CHUNK, (0, 18), *args)
            pump(8 * n + j + FLIGHT)
            yield j

    flat_in = inp.reshape(NO * NX * NY, 128)
    for i, k in enumerate((0, 3, 1, 2)):
        loads[k].wait()

        @pl.loop(8 * k, 8 * k + 8)
        def _(x):
            for y in range(NY):
                e0[HALO + x, HALO + y] = flat_in[pl.ds(x * NY + y, 8, stride=NX * NY), :]
        if i < 2:
            pump(i + 1)
            send_x(0, e0, i)
    pack_z(0, e0, 0)
    pack_z(0, e0, 1)
    pump(3)
    pot_load.wait()

    @pl.loop(0, NX)
    def _(x):
        for y in range(NY):
            potb[x, y] = jnp.broadcast_to(pot[x, pl.ds(y, 1)], (8, 128))

    first = (e0, e1, SIGMA1 / HALF, -SIGMA1 / HALF * MIDDLE, None, 0.0)
    interior(0, *first)
    z_halo(0, 1)
    pack_z(1, e1, 0)

    @pl.loop(0, 16)
    def _(x):
        for y in range(NY):
            one, two = potb[x, y], potb[16 + x, y]
            low = jnp.where(lane < 64, one, pltpu.roll(two, 64, axis=1))
            high = jnp.where(lane < 64, pltpu.roll(one, 64, axis=1), two)
            potp[x, y] = jnp.where(is_a, low, high)

    for j in faces(0, *first):
        if j == 1:
            send_x(1, e1, 0)
        if j == 3:
            send_x(1, e1, 1)
    pack_z(1, e1, 1)

    def pack_rows(lo, hi, rows):
        @pl.loop(lo, hi)
        def _(x):
            for y, n in rows:
                for j in range(y, y + n):
                    one, two = e2[HALO + x, HALO + j], e2[HALO + 16 + x, HALO + j]
                    low = jnp.where(lane < 64, one, pltpu.roll(two, 64, axis=1))
                    high = jnp.where(lane < 64, pltpu.roll(one, 64, axis=1), two)
                    pf[0, x, j] = jnp.where(is_a, low, high)
                    sb[x, j] = jnp.where(is_a, high, low)

    def piece(c, r):
        return pl.ds(4 * c, 4), pl.ds(*ROWS[r])

    def chip_copy(c, r):
        p = piece(c, r)
        return pltpu.make_async_remote_copy(
            src_ref=sb.at[p], dst_ref=pf.at[(1,) + p], send_sem=g_ss.at[c, r], recv_sem=g_rs.at[c, r],
            device_id=other_chip, device_id_type=MESH)

    def core_copy(s, c, r):
        p = (s,) + piece(c, r)
        return pltpu.make_async_remote_copy(
            src_ref=pf.at[p], dst_ref=ocp.at[p], send_sem=c_ss.at[s, c, r], recv_sem=c_rs.at[s, c, r],
            device_id=other_core, device_id_type=MESH)

    def ty_copy(s, c):
        xs = pl.ds(4 * c, 4)
        return pltpu.make_async_remote_copy(
            src_ref=pf.at[s, xs, pl.ds(0, HALO)], dst_ref=pf.at[s, xs, pl.ds(NY, HALO)],
            send_sem=ty_ss.at[s, c], recv_sem=ty_rs.at[s, c], device_id=lower["y"], device_id_type=MESH)

    def tx_copy(s, r):
        rows = pl.ds(*ROWS[r])
        return pltpu.make_async_remote_copy(
            src_ref=pf.at[s, pl.ds(0, HALO), rows], dst_ref=tx.at[s, :, rows],
            send_sem=tx_ss.at[s, r], recv_sem=tx_rs.at[s, r], device_id=lower["x"], device_id_type=MESH)

    def zp_copy(src, slot, dev):
        return pltpu.make_async_remote_copy(
            src_ref=zs.at[src], dst_ref=zp.at[slot], send_sem=zp_ss.at[src], recv_sem=zp_rs.at[slot],
            device_id=dev, device_id_type=MESH)

    def down(s, c, r):
        if r == 1:
            when(has_lower["y"], lambda: ty_copy(s, c).start())
        if c == 1:
            when(has_lower["x"], lambda: tx_copy(s, r).start())
        core_copy(s, c, r).start()

    def arrived(c, r):
        chip_copy(c, r).wait_recv()
        down(1, c, r)

    s2 = 2.0 * SIGMA2 / HALF
    second = (e1, e2, s2, -s2 * MIDDLE, e0, SIGMA1 * SIGMA2)
    interior(1, *second)
    pack_rows(0, 16, ROWS[:1])
    for c in range(4):
        chip_copy(c, 0).start()
    for c in range(4):
        down(0, c, 0)
    z_halo(1, 1)

    for j in faces(1, *second):
        if j % 2:
            c = j // 2
            pack_rows(4 * c, 4 * c + 4, ROWS[1:])
            for r in (1, 2):
                chip_copy(c, r).start()
            for r in (1, 2):
                down(0, c, r)
        if j == 4:
            arrived(0, 0)
            arrived(1, 0)
        if j == 6:
            arrived(2, 0)
            arrived(3, 0)
            arrived(0, 1)
            arrived(0, 2)
        if j == 7:
            arrived(1, 1)
            arrived(1, 2)

    @pl.when(is_a)
    def _():
        pack_top(64, zp, 0)

        @pl.when(bz == 1)
        def _():
            pack_top(0, zs, 1)
            zp_copy(1, 1, crossed).start()

    @pl.when(is_b)
    def _():
        pack_top(64, zs, 0)
        zp_copy(0, 1, other_chip).start()

        @pl.when(bz == 1)
        def _():
            pack_top(0, zs, 1)
            zp_copy(1, 0, (d - 1, o)).start()

    for c in (2, 3):
        for r in (1, 2):
            arrived(c, r)

    @pl.loop(0, NX)
    def _(x):
        for orb in range(NO):
            inp[orb, x] = e2[HALO + x, pl.ds(HALO, NY), orb]
    out_copy = pltpu.make_async_copy(inp, out_hbm.at[:, 0], out_sem)
    out_copy.start()

    def z_upper(s):
        @pl.loop(0, 4)
        def _(t):
            v = pf[s, pl.ds(4 * t, 4), pl.ds(0, NY)].reshape(4 * NY * 8, 128)
            parts = []
            for j in range(4):
                x = 4 * t + j
                packed = zp[s, x // 8].reshape(NY * 8, 128)
                parts.append(pltpu.roll(packed, lax.rem(128 - 16 * lax.rem(x, 8), 128), axis=1))
            r = jnp.dot(split_wide(v), zmat_ref[3], preferred_element_type=F32)
            r += jnp.dot(split_wide(jnp.concatenate(parts, axis=0)), zmat_ref[4], preferred_element_type=F32)
            zacc[pl.ds(16 * s + 4 * t, 4)] = (r[:, :128] + r[:, 128:]).reshape(4, NY, 8, 128)

    def shift_x(s):
        @pl.loop(0, HALO)
        def _(x):
            for y in range(NY):
                both = jnp.where(lane < 64, tx[s, x, y], pf[s, x, y])
                pf[s, 16 + x, y] = pltpu.roll(both, 64, axis=1)

    def half_rows(s, ys_):
        @pl.loop(0, 16)
        def _(x):
            for y in ys_:
                total = zacc[16 * s + x, pl.ds(y, HALO)]
                total += (0.5 * CENTRE + 0.5 * potp[x, pl.ds(y, HALO)]) * pf[s, x, pl.ds(y, HALO)]
                for m in range(1, HALO + 1):
                    near = pf[s, x + m, pl.ds(y, HALO)] + pf[s, x, pl.ds(y + m, HALO)]
                    total += (KINETIC * WEIGHTS[m - 1]) * near
                hp[s, x, pl.ds(y, HALO)] = total

    @pl.when(is_a)
    def _():
        zp_copy(0, 1, other_chip).wait_recv()

    @pl.when(is_b & (bz == 0))
    def _():
        zp_copy(1, 0, other_chip).wait_recv()
        zp_copy(1, 1, other_chip).wait_recv()

    for s in (0, 1):
        z_upper(s)
        for r in range(3):
            when(has_upper["x"], lambda: tx_copy(s, r).wait_recv())
        shift_x(s)
        half_rows(s, (0, 6, 12))
        for c in range(4):
            when(has_upper["y"], lambda: ty_copy(s, c).wait_recv())
        half_rows(s, (18,))

    for s in (0, 1):
        for c in range(4):
            for r in range(3):
                core_copy(s, c, r).wait_recv()

    def grams(x, total):
        mine = [flat(pf[s, x, pl.ds(0, NY)]) for s in (0, 1)]
        left = jnp.concatenate(mine + [flat(ocp[s, x]) for s in (0, 1)], axis=0)
        right = jnp.concatenate(mine + [flat(hp[s, x]) for s in (0, 1)], axis=0)
        return total + gram(left, right)

    def place(block, starts):
        n = block.shape[1]
        r = lax.broadcasted_iota(jnp.int32, (n, 128), 0)
        c = lax.broadcasted_iota(jnp.int32, (n, 128), 1)
        chosen = jnp.zeros((n, 128), jnp.bool_)
        for j, s in enumerate(starts):
            chosen = chosen | ((r // 8 == j) & (c == s + r % 8))
        return jnp.dot(block, chosen.astype(F32), precision=HIGH, preferred_element_type=F32)

    o_core = o + 1 - 2 * core
    o_chip = (o + 2) % 4
    placed = place(lax.fori_loop(0, 16, grams, jnp.zeros((32, 32), F32)),
                   (8 * o, 8 * o_chip, 32 + 8 * o, 32 + 8 * o_chip))
    for j, orbital in enumerate((o, o_chip, o_core, o_core + 2 - 4 * chip)):
        part[pl.ds(pl.multiple_of(8 * orbital, 8), 8), :] = placed[8 * j:8 * j + 8]

    def reduce(block, ar, ss, rs, mine, source, partners):
        ar[mine] = block
        copies = []
        for i, dev in enumerate(partners):
            copies.append(pltpu.make_async_remote_copy(
                src_ref=ar.at[mine], dst_ref=ar.at[mine], send_sem=ss.at[i], recv_sem=rs.at[mine],
                device_id=dev, device_id_type=MESH))
            copies[-1].start()
        for i, dev in enumerate(partners):
            at = source(i + 1)
            pltpu.make_async_remote_copy(
                src_ref=ar.at[at], dst_ref=ar.at[at], send_sem=ss.at[i], recv_sem=rs.at[at],
                device_id=dev, device_id_type=MESH).wait_recv()
        total = ar[0]
        for i in range(1, len(partners) + 1):
            total += ar[i]
        for c in copies:
            c.wait_send()
        return total

    folded = part[0:16, :] + pltpu.roll(part[16:32, :], 64, axis=1)
    folded = reduce(folded, ar1, a1_ss, a1_rs, 4 * pzl + o,
                    lambda i: 4 * ((pzl + i // 4) % 2) + (o + i) % 4, columns)
    folded = reduce(folded, ar2, a2_ss, a2_rs, 4 * bx + px,
                    lambda i: 4 * ((bx + i // 4) % 4) + (px + i) % 4, planes)
    part[0:16, :] = folded
    part[16:32, :] = pltpu.roll(folded, 64, axis=1)

    square = part[...]
    r = lax.broadcasted_iota(jnp.int32, (32, 32), 0)
    c = lax.broadcasted_iota(jnp.int32, (32, 32), 1)
    eye = (r == c).astype(F32)
    cor_ref[...] = square[:, 0:32] * (1.0 / CELLS)
    m = square[:, 32:64]
    t = lax.dot_general(m, eye, (((0,), (0,)), ((), ())), precision=HIGH, preferred_element_type=F32)
    sub_ref[...] = (m + t) * (1.0 / (CELLS * HALF))

    out_copy.wait()
    for q in range(len(queue) - FLIGHT, len(queue)):
        for side in (0, 1):
            when(sends("y", side), lambda: y_copy(*queue[q], side).wait_send())
    for n, buf in ((0, e0), (1, e1)):
        for side in (0, 1):
            when(sends("x", side), lambda: x_copy(n, buf, side).wait_send())
        for part_ in (0, 1):
            for copy in z_copies(n, part_):
                copy.wait_send()
    for c in range(4):
        for r in range(3):
            chip_copy(c, r).wait_send()
            for s in (0, 1):
                core_copy(s, c, r).wait_send()
        for s in (0, 1):
            when(has_lower["y"], lambda: ty_copy(s, c).wait_send())
    for s in (0, 1):
        for r in range(3):
            when(has_lower["x"], lambda: tx_copy(s, r).wait_send())
    when(is_b, lambda: zp_copy(0, 1, other_chip).wait_send())
    when(bz == 1, lambda: zp_copy(1, 1, other_chip).wait_send())


def shards(orbitals, potential):
    zmat = jnp.asarray(z_matrices())
    field = (NX + 12, NY + 12, 8, 128)
    vm = lambda *shape: pltpu.VMEM(shape, F32)
    dma = lambda *shape: pltpu.SemaphoreType.DMA(shape)
    out, cor, sub = pl.pallas_call(
        kernel,
        out_shape=(
            jax.ShapeDtypeStruct((NO, 1, NX, NY, NZ), F32),
            jax.ShapeDtypeStruct((32, 32), F32),
            jax.ShapeDtypeStruct((32, 32), F32),
        ),
        in_specs=[pl.BlockSpec(memory_space=pl.ANY)] * 2 + [pl.BlockSpec(memory_space=pltpu.VMEM)],
        out_specs=(pl.BlockSpec(memory_space=pl.ANY),) + (pl.BlockSpec(memory_space=pltpu.VMEM),) * 2,
        scratch_shapes=[
            vm(NO, NX, NY, NZ), vm(NX, NY, NZ), vm(*field), vm(*field), vm(*field),
            vm(NX, NY, 8, 128), vm(NX, NY, 8, 128),
            vm(2, 2, NY, 8, 128), vm(2, 2, NY, 8, 128),
            vm(2, 16 + HALO, NY + HALO, 8, 128), vm(16, NY, 8, 128), vm(2, 16, NY, 8, 128),
            vm(2, 16, NY, 8, 128), vm(2, HALO, NY, 8, 128), vm(16, NY, 8, 128),
            vm(2, 2, NY, 8, 128), vm(2, 2, NY, 8, 128),
            vm(32, 128), vm(8, 16, 128), vm(16, 16, 128),
            dma(4), pltpu.SemaphoreType.DMA, pltpu.SemaphoreType.DMA,
            dma(2, 8, 2), dma(2, 8, 2), dma(2, 2), dma(2, 2), dma(2, 3), dma(2, 3),
            dma(2, 4, 3), dma(2, 4, 3), dma(4, 3), dma(4, 3),
            dma(2, 4), dma(2, 4), dma(2, 3), dma(2, 3), dma(2), dma(2),
            dma(7), dma(8), dma(15), dma(16),
        ],
        compiler_params=pltpu.CompilerParams(
            collective_id=0, has_side_effects=True, vmem_limit_bytes=58 * 2**20),
        name="filter_and_subspace",
    )(orbitals, potential, zmat)
    return out, cor, sub


def solution(mesh):
    placed = (P("orb", "dom", None, None, None), P("dom", None, None, None))
    return jax.shard_map(
        shards,
        mesh=mesh,
        in_specs=placed,
        out_specs=(P("orb", "dom", None, None, None), P(), P()),
        check_vma=False,
    )
```

time: 190 us -> 158 us (0.83); the launches traced: 188 us -> 158 us
  Pallas kernels: 182 us -> 153 us
    pallas_call x1, Pallas kernels: 182 us -> 153 us  [shards(): pl.pallas_call(kernel, out_shape=(jax.ShapeDtypeStruct((NO, 1, NX, NY, NZ...]
where the time goes in v2:
time: 158 us
  Pallas kernels  153 us (97%)
  local copies, waits for them, and re-layouts  5.01 us (3%)
    pallas_call x1, Pallas kernels, shards(): pl.pallas_call(kernel, out_shape=(jax.ShapeDtypeStruct((NO, 1, NX, NY, NZ...  153 us
    unnamed x7, local copies, waits for them, and re-layouts  5.01 us

profile of v2, /device:TPU:1, one launch (start us, length us, event | category | flops | bytes accessed | tf_op | source)
XLA Modules:
  0.0 158.2 jit_solution(4652392755146301965)
XLA Ops:
  0.6 152.5 %filter_and_subspace.1 = (f32[8,1,32,24,128]{4,3,2,1,0:T(8,128)}, f32[32,32]{1,0:T(8,128)}, f32[32,32]{1,0:T(8,128)}) custom-call(f32[8,1,32,24,128]{4,3,2,1,0:T(8,128)} %orb_hbm.1, f32[1,32,24,128]{3,2,1,0:T(8,128)} %pot_hbm.1, bf16[5,256,256]{2,1,0:T(8,128)(2,1)} %constant.2.clone.zmat_ref), custom_call_target="tpu_custom_call" | custom-call | tf_op jit(solution)/shard_map/filter_and_subspace/pallas_call | solution.py:653
  153.1 0.0 copy-start.1
  153.2 0.0 copy-start
  153.2 3.8 %copy.9 = f32[8,1,32,24,128]{4,3,2,1,0:T(8,128)} copy(f32[8,1,32,24,128]{4,3,2,1,0:T(8,128)} %get-tuple-element.6) | data formatting | bytes 6291456
  157.0 0.0 copy-done.1
  157.0 0.6 copy.10
  157.6 0.0 copy-done
  157.6 0.6 copy.11
Async XLA Ops:
  153.1 3.8 %copy-start.1 = (f32[32,32]{1,0:T(8,128)S(1)}, f32[32,32]{1,0:T(8,128)}, u32[]{:S(2)}) copy-start(f32[32,32]{1,0:T(8,128)} %get-tuple-element.7) | copy-start | bytes 12292
  153.2 4.4 %copy-start = (f32[32,32]{1,0:T(8,128)S(1)}, f32[32,32]{1,0:T(8,128)}, u32[]{:S(2)}) copy-start(f32[32,32]{1,0:T(8,128)} %get-tuple-element.8) | copy-start | bytes 12292

commit v3 on v2

--- a/solution.py
+++ b/solution.py
@@ -100,9 +100,9 @@
 
 
 def kernel(orb_hbm, pot_hbm, zmat_ref, out_hbm, cor_ref, sub_ref,
-           inp, pot, e0, e1, e2, zacc, potb, zf, zh, pf, sb, ocp, hp, tx, potp, zs, zp, part, ar1, ar2,
+           inp, pot, e0, e1, e2, zacc, potb, zf, zh, rl, pf, sb, ocp, hp, tp, tx, potp, zs, zp, part, ar1, ar2,
            in_sem, pot_sem, out_sem,
-           y_ss, y_rs, x_ss, x_rs, z_ss, z_rs, c_ss, c_rs, g_ss, g_rs,
+           y_ss, y_rs, r_ss, r_rs, p_ss, x_ss, x_rs, z_ss, z_rs, c_ss, c_rs, g_ss, g_rs,
            ty_ss, ty_rs, tx_ss, tx_rs, zp_ss, zp_rs, a1_ss, a1_rs, a2_ss, a2_rs):
     d = lax.axis_index("dom")
     o = lax.axis_index("orb")
@@ -115,6 +115,7 @@
     plane = lambda i: (((bx + i // 4) % 4) * 8 + 4 * pzl + (px + i) % 4, o)
     columns = [column(i) for i in range(1, 8)]
     planes = [plane(i) for i in range(1, 16)]
+    zl = (d + 4 - 8 * pzl, o)
     crossed = (d + 1 - 2 * bz, (o + 2) % 4)
     lower = {"x": (d - 8, o), "y": (d - 2, o)}
     upper = {"x": (d + 8, o), "y": (d + 2, o)}
@@ -226,17 +227,52 @@
         return (has_upper, has_lower)[side][axis]
 
     queue = [(n, buf, k) for n, buf in ((0, e0), (1, e1)) for k in ORDERS[n]]
-    sent = []
+    sent, passed = [], []
+
+    def direct(q, side):
+        if q % 2 == 0:
+            return sends("y", side)
+        return ((by == 1) | (by == 3), (by == 0) | (by == 2))[side]
+
+    def relayed(q, side):
+        n, buf, k = queue[q]
+        return pltpu.make_async_remote_copy(
+            src_ref=buf.at[pl.ds(HALO + CHUNK * k, CHUNK), pl.ds((HALO, NY)[side], HALO)],
+            dst_ref=rl.at[n, q % 8 // 2], send_sem=r_ss.at[n, q % 8 // 2], recv_sem=r_rs.at[n, q % 8 // 2],
+            device_id=zl, device_id_type=MESH)
+
+    def passing(q, side):
+        n, buf, k = queue[q]
+        return pltpu.make_async_remote_copy(
+            src_ref=rl.at[n, q % 8 // 2],
+            dst_ref=buf.at[pl.ds(HALO + CHUNK * k, CHUNK), pl.ds((NY + HALO, 0)[side], HALO)],
+            send_sem=p_ss.at[n, q % 8 // 2], recv_sem=y_rs.at[n, k, side],
+            device_id=(upper, lower)[side]["y"], device_id_type=MESH)
+
+    def each_send(q, act):
+        for side in (0, 1):
+            when(direct(q, side), lambda: act(y_copy(*queue[q], side)))
+            if q % 2:
+                when(by == 2 - side, lambda: act(relayed(q, side)))
+
+    def pass_on(q):
+        for side in (0, 1):
+            def go():
+                relayed(q, side).wait_recv()
+                passing(q, side).start()
+            when(by == 3 * side, go)
 
     def pump(last):
         while len(sent) <= min(last, len(queue) - 1):
             q = len(sent)
             if q >= FLIGHT:
-                for side in (0, 1):
-                    when(sends("y", side), lambda: y_copy(*queue[q - FLIGHT], side).wait_send())
-            for side in (0, 1):
-                when(sends("y", side), lambda: y_copy(*queue[q], side).start())
+                each_send(q - FLIGHT, lambda c: c.wait_send())
+            each_send(q, lambda c: c.start())
             sent.append(q)
+        while 2 * len(passed) + 1 < min(last, len(queue)):
+            q = 2 * len(passed) + 1
+            pass_on(q)
+            passed.append(q)
 
     def wait_y(q):
         for side in (0, 1):
@@ -425,11 +461,23 @@
             src_ref=pf.at[s, xs, pl.ds(0, HALO)], dst_ref=pf.at[s, xs, pl.ds(NY, HALO)],
             send_sem=ty_ss.at[s, c], recv_sem=ty_rs.at[s, c], device_id=lower["y"], device_id_type=MESH)
 
-    def tx_copy(s, r):
-        rows = pl.ds(*ROWS[r])
-        return pltpu.make_async_remote_copy(
-            src_ref=pf.at[s, pl.ds(0, HALO), rows], dst_ref=tx.at[s, :, rows],
-            send_sem=tx_ss.at[s, r], recv_sem=tx_rs.at[s, r], device_id=lower["x"], device_id_type=MESH)
+    PAIRS = ((6, 12), (0, 18))
+
+    def tx_copy(s, half):
+        rows = pl.ds(6 * half, 6)
+        return pltpu.make_async_remote_copy(
+            src_ref=tp.at[s, :, rows], dst_ref=tx.at[s, :, rows],
+            send_sem=tx_ss.at[s, half], recv_sem=tx_rs.at[s, half], device_id=lower["x"], device_id_type=MESH)
+
+    def send_tx(s, half):
+        one, two = PAIRS[half]
+
+        @pl.loop(0, HALO)
+        def _(x):
+            for j in range(6):
+                tp[s, x, 6 * half + j] = jnp.where(
+                    lane < 64, pf[s, x, one + j], pltpu.roll(pf[s, x, two + j], 64, axis=1))
+        when(has_lower["x"], lambda: tx_copy(s, half).start())
 
     def zp_copy(src, slot, dev):
         return pltpu.make_async_remote_copy(
@@ -439,8 +487,8 @@
     def down(s, c, r):
         if r == 1:
             when(has_lower["y"], lambda: ty_copy(s, c).start())
-        if c == 1:
-            when(has_lower["x"], lambda: tx_copy(s, r).start())
+        if c == 1 and r != 1:
+            send_tx(s, r // 2)
         core_copy(s, c, r).start()
 
     def arrived(c, r):
@@ -523,9 +571,13 @@
     def shift_x(s):
         @pl.loop(0, HALO)
         def _(x):
-            for y in range(NY):
-                both = jnp.where(lane < 64, tx[s, x, y], pf[s, x, y])
-                pf[s, 16 + x, y] = pltpu.roll(both, 64, axis=1)
+            for half, (one, two) in enumerate(PAIRS):
+                for j in range(6):
+                    there = tx[s, x, 6 * half + j]
+                    both = jnp.where(lane < 64, there, pf[s, x, one + j])
+                    pf[s, 16 + x, one + j] = pltpu.roll(both, 64, axis=1)
+                    pf[s, 16 + x, two + j] = jnp.where(
+                        lane < 64, pltpu.roll(pf[s, x, two + j], 64, axis=1), there)
 
     def half_rows(s, ys_):
         @pl.loop(0, 16)
@@ -549,24 +601,30 @@
 
     for s in (0, 1):
         z_upper(s)
-        for r in range(3):
-            when(has_upper["x"], lambda: tx_copy(s, r).wait_recv())
+        for half in (0, 1):
+            when(has_upper["x"], lambda: tx_copy(s, half).wait_recv())
         shift_x(s)
         half_rows(s, (0, 6, 12))
-        for c in range(4):
-            when(has_upper["y"], lambda: ty_copy(s, c).wait_recv())
-        half_rows(s, (18,))
 
     for s in (0, 1):
         for c in range(4):
             for r in range(3):
                 core_copy(s, c, r).wait_recv()
 
-    def grams(x, total):
-        mine = [flat(pf[s, x, pl.ds(0, NY)]) for s in (0, 1)]
-        left = jnp.concatenate(mine + [flat(ocp[s, x]) for s in (0, 1)], axis=0)
-        right = jnp.concatenate(mine + [flat(hp[s, x]) for s in (0, 1)], axis=0)
-        return total + gram(left, right)
+    def grams(rows):
+        def body(x, total):
+            mine = [flat(pf[s, x, rows]) for s in (0, 1)]
+            left = jnp.concatenate(mine + [flat(ocp[s, x, rows]) for s in (0, 1)], axis=0)
+            right = jnp.concatenate(mine + [flat(hp[s, x, rows]) for s in (0, 1)], axis=0)
+            return total + gram(left, right)
+        return body
+
+    total = lax.fori_loop(0, 16, grams(pl.ds(0, 18)), jnp.zeros((32, 32), F32))
+    for s in (0, 1):
+        for c in range(4):
+            when(has_upper["y"], lambda: ty_copy(s, c).wait_recv())
+        half_rows(s, (18,))
+    total = lax.fori_loop(0, 16, grams(pl.ds(18, 6)), total)
 
     def place(block, starts):
         n = block.shape[1]
@@ -579,8 +637,7 @@
 
     o_core = o + 1 - 2 * core
     o_chip = (o + 2) % 4
-    placed = place(lax.fori_loop(0, 16, grams, jnp.zeros((32, 32), F32)),
-                   (8 * o, 8 * o_chip, 32 + 8 * o, 32 + 8 * o_chip))
+    placed = place(total, (8 * o, 8 * o_chip, 32 + 8 * o, 32 + 8 * o_chip))
     for j, orbital in enumerate((o, o_chip, o_core, o_core + 2 - 4 * chip)):
         part[pl.ds(pl.multiple_of(8 * orbital, 8), 8), :] = placed[8 * j:8 * j + 8]
 
@@ -623,8 +680,10 @@
 
     out_copy.wait()
     for q in range(len(queue) - FLIGHT, len(queue)):
+        each_send(q, lambda c: c.wait_send())
+    for q in passed:
         for side in (0, 1):
-            when(sends("y", side), lambda: y_copy(*queue[q], side).wait_send())
+            when(by == 3 * side, lambda: passing(q, side).wait_send())
     for n, buf in ((0, e0), (1, e1)):
         for side in (0, 1):
             when(sends("x", side), lambda: x_copy(n, buf, side).wait_send())
@@ -639,8 +698,8 @@
         for s in (0, 1):
             when(has_lower["y"], lambda: ty_copy(s, c).wait_send())
     for s in (0, 1):
-        for r in range(3):
-            when(has_lower["x"], lambda: tx_copy(s, r).wait_send())
+        for half in (0, 1):
+            when(has_lower["x"], lambda: tx_copy(s, half).wait_send())
     when(is_b, lambda: zp_copy(0, 1, other_chip).wait_send())
     when(bz == 1, lambda: zp_copy(1, 1, other_chip).wait_send())
 
@@ -662,13 +721,13 @@
         scratch_shapes=[
             vm(NO, NX, NY, NZ), vm(NX, NY, NZ), vm(*field), vm(*field), vm(*field),
             vm(NX, NY, 8, 128), vm(NX, NY, 8, 128),
-            vm(2, 2, NY, 8, 128), vm(2, 2, NY, 8, 128),
+            vm(2, 2, NY, 8, 128), vm(2, 2, NY, 8, 128), vm(2, 4, CHUNK, HALO, 8, 128),
             vm(2, 16 + HALO, NY + HALO, 8, 128), vm(16, NY, 8, 128), vm(2, 16, NY, 8, 128),
-            vm(2, 16, NY, 8, 128), vm(2, HALO, NY, 8, 128), vm(16, NY, 8, 128),
+            vm(2, 16, NY, 8, 128), vm(2, HALO, 12, 8, 128), vm(2, HALO, 12, 8, 128), vm(16, NY, 8, 128),
             vm(2, 2, NY, 8, 128), vm(2, 2, NY, 8, 128),
             vm(32, 128), vm(8, 16, 128), vm(16, 16, 128),
             dma(4), pltpu.SemaphoreType.DMA, pltpu.SemaphoreType.DMA,
-            dma(2, 8, 2), dma(2, 8, 2), dma(2, 2), dma(2, 2), dma(2, 3), dma(2, 3),
+            dma(2, 8, 2), dma(2, 8, 2), dma(2, 4), dma(2, 4), dma(2, 4), dma(2, 2), dma(2, 2), dma(2, 3), dma(2, 3),
             dma(2, 4, 3), dma(2, 4, 3), dma(4, 3), dma(4, 3),
             dma(2, 4), dma(2, 4), dma(2, 3), dma(2, 3), dma(2), dma(2),
             dma(7), dma(8), dma(15), dma(16),

time: 158 us -> 148 us (0.937)
  Pallas kernels: 153 us -> 143 us
    pallas_call x1, Pallas kernels: 153 us -> 143 us  [shards(): pl.pallas_call(kernel, out_shape=(jax.ShapeDtypeStruct((NO, 1, NX, NY, NZ...]
where the time goes in v3:
time: 148 us
  Pallas kernels  143 us (97%)
  local copies, waits for them, and re-layouts  5.01 us (3%)
    pallas_call x1, Pallas kernels, shards(): pl.pallas_call(kernel, out_shape=(jax.ShapeDtypeStruct((NO, 1, NX, NY, NZ...  143 us
    unnamed x7, local copies, waits for them, and re-layouts  5.01 us

profile of v3, /device:TPU:1, one launch (start us, length us, event | category | flops | bytes accessed | tf_op | source)
XLA Modules:
  0.0 148.3 jit_solution(4717572625474456441)
XLA Ops:
  0.6 142.6 %filter_and_subspace.1 = (f32[8,1,32,24,128]{4,3,2,1,0:T(8,128)}, f32[32,32]{1,0:T(8,128)}, f32[32,32]{1,0:T(8,128)}) custom-call(f32[8,1,32,24,128]{4,3,2,1,0:T(8,128)} %orb_hbm.1, f32[1,32,24,128]{3,2,1,0:T(8,128)} %pot_hbm.1, bf16[5,256,256]{2,1,0:T(8,128)(2,1)} %constant.2.clone.zmat_ref), custom_call_target="tpu_custom_call" | custom-call | tf_op jit(solution)/shard_map/filter_and_subspace/pallas_call | solution.py:712
  143.3 0.0 copy-start.1
  143.3 0.0 copy-start
  143.3 3.8 %copy.9 = f32[8,1,32,24,128]{4,3,2,1,0:T(8,128)} copy(f32[8,1,32,24,128]{4,3,2,1,0:T(8,128)} %get-tuple-element.6) | data formatting | bytes 6291456
  147.1 0.0 copy-done.1
  147.1 0.6 copy.10
  147.7 0.0 copy-done
  147.7 0.6 copy.11
Async XLA Ops:
  143.3 3.8 %copy-start.1 = (f32[32,32]{1,0:T(8,128)S(1)}, f32[32,32]{1,0:T(8,128)}, u32[]{:S(2)}) copy-start(f32[32,32]{1,0:T(8,128)} %get-tuple-element.7) | copy-start | bytes 12292
  143.3 4.4 %copy-start = (f32[32,32]{1,0:T(8,128)S(1)}, f32[32,32]{1,0:T(8,128)}, u32[]{:S(2)}) copy-start(f32[32,32]{1,0:T(8,128)} %get-tuple-element.8) | copy-start | bytes 12292

commit v4 on v3

--- a/solution.py
+++ b/solution.py
@@ -16,9 +16,11 @@
 NX, NY, NZ, NO = 32, 24, 128, 8
 CELLS = 3145728
 CHUNK = 4
-ORDERS = ((0, 1, 7, 6, 4, 5, 2, 3), (0, 4, 1, 5, 2, 6, 3, 7))
-FLIGHT = 3
+ORDERS = ((3, 7, 2, 6, 0, 4, 1, 5), (0, 4, 1, 5, 3, 7, 2, 6))
+FLIGHT = 4
+LOADS = (1, 3, 0, 2)
 ROWS = ((6, 12), (0, 6), (18, 6))
+PARTS = ((0,), (1, 2))
 MESH = pl.DeviceIdType.MESH
 F32, BF16 = jnp.float32, jnp.bfloat16
 HIGH = lax.Precision.HIGHEST
@@ -82,19 +84,6 @@
     return jnp.concatenate([hi, lo], axis=1)
 
 
-def split_tall(v):
-    hi = v.astype(BF16).astype(F32)
-    return jnp.concatenate([hi, v - hi], axis=0).astype(BF16)
-
-
-def gram(left, right):
-    rows, cols = left.shape[0], right.shape[0]
-    full = lax.dot_general(
-        split_tall(left), split_tall(right), (((1,), (1,)), ((), ())), preferred_element_type=F32
-    )
-    return (full[:rows, :cols] + full[rows:, :cols]) + (full[:rows, cols:] + full[rows:, cols:])
-
-
 def flat(block):
     return jnp.concatenate([block[j] for j in range(block.shape[0])], axis=1)
 
@@ -134,7 +123,7 @@
             orb_hbm.at[:, 0, pl.ds(8 * k, 8)], inp.at[:, pl.ds(8 * k, 8)], in_sem.at[k])
         for k in range(4)
     ]
-    for k in (0, 3, 1, 2):
+    for k in LOADS:
         loads[k].start()
     pot_load = pltpu.make_async_copy(pot_hbm.at[0], pot, pot_sem)
     pot_load.start()
@@ -203,12 +192,12 @@
             send_sem=y_ss.at[stage, k, side], recv_sem=y_rs.at[stage, k, side],
             device_id=(lower, upper)[side]["y"], device_id_type=MESH)
 
-    def x_copy(stage, buf, side):
+    def x_copy(stage, buf, side, r):
         src, dst = ((HALO, NX + HALO), (NX, 0))[side]
-        cols = pl.ds(HALO, NY)
+        cols = pl.ds(HALO + ROWS[r][0], ROWS[r][1])
         return pltpu.make_async_remote_copy(
             src_ref=buf.at[pl.ds(src, HALO), cols], dst_ref=buf.at[pl.ds(dst, HALO), cols],
-            send_sem=x_ss.at[stage, side], recv_sem=x_rs.at[stage, side],
+            send_sem=x_ss.at[stage, side, r], recv_sem=x_rs.at[stage, side, r],
             device_id=(lower, upper)[side]["x"], device_id_type=MESH)
 
     def z_copies(stage, part):
@@ -217,7 +206,7 @@
                 src_ref=zf.at[stage, :, pl.ds(*ROWS[r])], dst_ref=zh.at[stage, :, pl.ds(*ROWS[r])],
                 send_sem=z_ss.at[stage, r], recv_sem=z_rs.at[stage, r],
                 device_id=(d + 1 - 2 * bz, o), device_id_type=MESH)
-            for r in ((0,), (1, 2))[part]
+            for r in PARTS[part]
         ]
 
     def sends(axis, side):
@@ -262,14 +251,17 @@
                 passing(q, side).start()
             when(by == 3 * side, go)
 
-    def pump(last):
+    def pump(last, done=-1):
         while len(sent) <= min(last, len(queue) - 1):
             q = len(sent)
+            if q >= 8 and ORDERS[0].index(queue[q][2]) > done:
+                break
             if q >= FLIGHT:
                 each_send(q - FLIGHT, lambda c: c.wait_send())
             each_send(q, lambda c: c.start())
             sent.append(q)
-        while 2 * len(passed) + 1 < min(last, len(queue)):
+        while 2 * len(passed) + 1 < min(len(sent) - 1, last) or (
+                last >= len(queue) and len(sent) == len(queue) and len(passed) < 8):
             q = 2 * len(passed) + 1
             pass_on(q)
             passed.append(q)
@@ -278,12 +270,14 @@
         for side in (0, 1):
             when(receives("y", side), lambda: y_copy(*queue[q], side).wait_recv())
 
-    def send_x(stage, buf, side):
-        when(sends("x", side), lambda: x_copy(stage, buf, side).start())
-
-    def wait_x(stage, buf):
+    def send_x(stage, buf, side, part):
+        for r in PARTS[part]:
+            when(sends("x", side), lambda: x_copy(stage, buf, side, r).start())
+
+    def wait_x(stage, buf, part):
         for side in (0, 1):
-            when(receives("x", side), lambda: x_copy(stage, buf, side).wait_recv())
+            for r in PARTS[part]:
+                when(receives("x", side), lambda: x_copy(stage, buf, side, r).wait_recv())
 
     lane = lax.broadcasted_iota(jnp.int32, (8, 128), 1)
 
@@ -308,26 +302,31 @@
         for copy in z_copies(stage, part):
             copy.start()
 
-    def pack_top(first, dst, slot):
-        @pl.loop(0, 2)
-        def _(half):
-            @pl.loop(0, NY // 4)
-            def _(t):
-                for j in range(4):
-                    total = None
-                    for i in range(16):
-                        moved = pltpu.roll(
-                            e2[HALO + 8 * half + i // 2 + 16 * (i % 2), HALO + 4 * t + j],
-                            (8 * i + 128 - first) % 128, axis=1)
-                        total = moved if total is None else jnp.where(lane // 8 == i, moved, total)
-                    dst[slot, half, 4 * t + j] = total
-
-    def z_own(buf):
+    def pack_top(first, dst, slot, half):
+        @pl.loop(0, NY // 4)
+        def _(t):
+            for j in range(4):
+                total = None
+                for i in range(16):
+                    moved = pltpu.roll(
+                        e2[8 * half + i // 2 + 16 * (i % 2), 4 * t + j],
+                        (8 * i + 128 - first) % 128, axis=1)
+                    total = moved if total is None else jnp.where(lane // 8 == i, moved, total)
+                dst[slot, half, 4 * t + j] = total
+
+    def z_own(buf, part):
         @pl.loop(0, NX // 4)
         def _(t):
-            v = buf[pl.ds(HALO + 4 * t, 4), pl.ds(HALO, NY)].reshape(4 * NY * 8, 128)
-            r = jnp.dot(split_wide(v), zmat_ref[0], preferred_element_type=F32)
-            zacc[pl.ds(4 * t, 4)] = (r[:, :128] + r[:, 128:]).reshape(4, NY, 8, 128)
+            at = pl.ds(4 * t, 4)
+            v = [buf[pl.ds(HALO + 4 * t, 4), pl.ds(HALO + ROWS[r][0], ROWS[r][1])] for r in PARTS[part]]
+            v = jnp.concatenate(v, axis=1) if part else v[0]
+            r = jnp.dot(split_wide(v.reshape(4 * 12 * 8, 128)), zmat_ref[0], preferred_element_type=F32)
+            r = (r[:, :128] + r[:, 128:]).reshape(4, 12, 8, 128)
+            if part == 0:
+                zacc[at, pl.ds(6, 12)] = r
+            else:
+                zacc[at, pl.ds(0, 6)] = r[:, :6]
+                zacc[at, pl.ds(18, 6)] = r[:, 6:]
 
     def z_halo(stage, part):
         for copy in z_copies(stage, part):
@@ -339,7 +338,7 @@
             for j in range(4):
                 x = 4 * t + j
                 packed = [zh[stage, x // 16, pl.ds(*ROWS[r])].reshape(ROWS[r][1] * 8, 128)
-                          for r in ((0,), (1, 2))[part]]
+                          for r in PARTS[part]]
                 packed = jnp.concatenate(packed, axis=0) if part else packed[0]
                 parts.append(pltpu.roll(packed, lax.rem(128 - 8 * lax.rem(x, 16), 128), axis=1))
             v = jnp.concatenate(parts, axis=0)
@@ -352,7 +351,7 @@
                 zacc[at, pl.ds(0, 6)] += r[:, :6]
                 zacc[at, pl.ds(18, 6)] += r[:, 6:]
 
-    def rows_of(src, dst, x, y, scale, shift, prev, prev_scale):
+    def rows_of(src, dst, off, x, y, scale, shift, prev, prev_scale):
         def at(dx, dy):
             return src[x + HALO + dx, pl.ds(y + HALO + dy, HALO)]
 
@@ -363,33 +362,23 @@
             total += (scale * KINETIC * WEIGHTS[m - 1]) * near
         if prev is not None:
             total -= prev_scale * prev[x + HALO, pl.ds(y + HALO, HALO)]
-        dst[x + HALO, pl.ds(y + HALO, HALO)] = total
+        dst[x + off, pl.ds(y + off, HALO)] = total
 
     def stage_rows(lo, hi, ys_, *args):
         @pl.loop(lo, hi)
         def _(x):
             for y in ys_:
-                rows_of(args[0], args[1], x, y, *args[2:])
-
-    def interior(n, src, *args):
-        z_own(src)
-        pump(8 * n + 4 - n)
-        z_halo(n, 0)
-        stage_rows(HALO, NX - HALO, (6, 12), src, *args)
-        pump(8 * n + 5 - 2 * n)
-        wait_x(n, src)
-        stage_rows(0, HALO, (6, 12), src, *args)
-        stage_rows(NX - HALO, NX, (6, 12), src, *args)
+                rows_of(*args[:3], x, y, *args[3:])
 
     def faces(n, *args):
         for j, k in enumerate(ORDERS[n]):
             wait_y(8 * n + j)
             stage_rows(CHUNK * k, CHUNK * k + CHUNK, (0, 18), *args)
-            pump(8 * n + j + FLIGHT)
-            yield j
+            pump(8 * n + j + FLIGHT, 8 * n + j)
+            yield j, k
 
     flat_in = inp.reshape(NO * NX * NY, 128)
-    for i, k in enumerate((0, 3, 1, 2)):
+    for i, k in enumerate(LOADS):
         loads[k].wait()
 
         @pl.loop(8 * k, 8 * k + 8)
@@ -397,8 +386,11 @@
             for y in range(NY):
                 e0[HALO + x, HALO + y] = flat_in[pl.ds(x * NY + y, 8, stride=NX * NY), :]
         if i < 2:
-            pump(i + 1)
-            send_x(0, e0, i)
+            pump(i)
+    for side in (0, 1):
+        for part_ in (0, 1):
+            send_x(0, e0, side, part_)
+    pump(2)
     pack_z(0, e0, 0)
     pack_z(0, e0, 1)
     pump(3)
@@ -409,10 +401,20 @@
         for y in range(NY):
             potb[x, y] = jnp.broadcast_to(pot[x, pl.ds(y, 1)], (8, 128))
 
-    first = (e0, e1, SIGMA1 / HALF, -SIGMA1 / HALF * MIDDLE, None, 0.0)
-    interior(0, *first)
+    first = (e0, e1, HALO, SIGMA1 / HALF, -SIGMA1 / HALF * MIDDLE, None, 0.0)
+    z_own(e0, 0)
+    z_own(e0, 1)
+    z_halo(0, 0)
+    stage_rows(HALO, NX - HALO, (6, 12), *first)
+    pump(4)
+    wait_x(0, e0, 0)
+    stage_rows(0, HALO, (6, 12), *first)
+    stage_rows(NX - HALO, NX, (6, 12), *first)
+    send_x(1, e1, 0, 0)
+    send_x(1, e1, 1, 0)
+    pack_z(1, e1, 0)
+    z_own(e1, 0)
     z_halo(0, 1)
-    pack_z(1, e1, 0)
 
     @pl.loop(0, 16)
     def _(x):
@@ -422,19 +424,16 @@
             high = jnp.where(lane < 64, pltpu.roll(one, 64, axis=1), two)
             potp[x, y] = jnp.where(is_a, low, high)
 
-    for j in faces(0, *first):
-        if j == 1:
-            send_x(1, e1, 0)
-        if j == 3:
-            send_x(1, e1, 1)
-    pack_z(1, e1, 1)
+    wait_x(0, e0, 1)
+    z_halo(1, 0)
+    wait_x(1, e1, 0)
 
     def pack_rows(lo, hi, rows):
         @pl.loop(lo, hi)
         def _(x):
             for y, n in rows:
                 for j in range(y, y + n):
-                    one, two = e2[HALO + x, HALO + j], e2[HALO + 16 + x, HALO + j]
+                    one, two = e2[x, j], e2[16 + x, j]
                     low = jnp.where(lane < 64, one, pltpu.roll(two, 64, axis=1))
                     high = jnp.where(lane < 64, pltpu.roll(one, 64, axis=1), two)
                     pf[0, x, j] = jnp.where(is_a, low, high)
@@ -496,64 +495,78 @@
         down(1, c, r)
 
     s2 = 2.0 * SIGMA2 / HALF
-    second = (e1, e2, s2, -s2 * MIDDLE, e0, SIGMA1 * SIGMA2)
-    interior(1, *second)
-    pack_rows(0, 16, ROWS[:1])
-    for c in range(4):
-        chip_copy(c, 0).start()
-    for c in range(4):
-        down(0, c, 0)
+    second = (e1, e2, 0, s2, -s2 * MIDDLE, e0, SIGMA1 * SIGMA2)
+    for j, k in faces(0, *first):
+        stage_rows(CHUNK * k, CHUNK * k + CHUNK, (6, 12), *second)
+        if j % 2:
+            c = k % 4
+            pack_rows(4 * c, 4 * c + 4, ROWS[:1])
+            chip_copy(c, 0).start()
+            down(0, c, 0)
+        if j == 3:
+            send_x(1, e1, 1, 1)
+        if j == 6:
+            send_x(1, e1, 0, 1)
+
+    def tops(half):
+        @pl.when(is_a)
+        def _():
+            pack_top(64, zp, 0, half)
+
+            @pl.when(bz == 1)
+            def _():
+                pack_top(0, zs, 1, half)
+
+        @pl.when(is_b)
+        def _():
+            pack_top(64, zs, 0, half)
+
+            @pl.when(bz == 1)
+            def _():
+                pack_top(0, zs, 1, half)
+
+    def leave(c):
+        @pl.loop(0, 2)
+        def _(g):
+            @pl.loop(0, CHUNK)
+            def _(x):
+                at = 16 * g + 4 * c + x
+                for orb in range(NO):
+                    inp[orb, at] = e2[at, :, orb]
+
+    pack_z(1, e1, 1)
+    z_own(e1, 1)
+    wait_x(1, e1, 1)
     z_halo(1, 1)
-
-    for j in faces(1, *second):
+    early = [(3, 0), (2, 0), (0, 0), (1, 0), (0, 1), (0, 2), (1, 1), (1, 2), (3, 1), (3, 2), (2, 1), (2, 2)]
+    for j, k in faces(1, *second):
         if j % 2:
-            c = j // 2
+            c = k % 4
             pack_rows(4 * c, 4 * c + 4, ROWS[1:])
             for r in (1, 2):
                 chip_copy(c, r).start()
             for r in (1, 2):
                 down(0, c, r)
-        if j == 4:
-            arrived(0, 0)
-            arrived(1, 0)
-        if j == 6:
-            arrived(2, 0)
-            arrived(3, 0)
-            arrived(0, 1)
-            arrived(0, 2)
-        if j == 7:
-            arrived(1, 1)
-            arrived(1, 2)
-
-    @pl.when(is_a)
-    def _():
-        pack_top(64, zp, 0)
-
-        @pl.when(bz == 1)
-        def _():
-            pack_top(0, zs, 1)
-            zp_copy(1, 1, crossed).start()
+            for _ in range(2):
+                arrived(*early.pop(0))
+
+            if c != 2:
+                leave(c)
+        if j == 3:
+            tops(0)
+    tops(1)
+
+    @pl.when(is_a & (bz == 1))
+    def _():
+        zp_copy(1, 1, crossed).start()
 
     @pl.when(is_b)
     def _():
-        pack_top(64, zs, 0)
         zp_copy(0, 1, other_chip).start()
 
-        @pl.when(bz == 1)
-        def _():
-            pack_top(0, zs, 1)
-            zp_copy(1, 0, (d - 1, o)).start()
-
-    for c in (2, 3):
-        for r in (1, 2):
-            arrived(c, r)
-
-    @pl.loop(0, NX)
-    def _(x):
-        for orb in range(NO):
-            inp[orb, x] = e2[HALO + x, pl.ds(HALO, NY), orb]
-    out_copy = pltpu.make_async_copy(inp, out_hbm.at[:, 0], out_sem)
-    out_copy.start()
+    @pl.when(is_b & (bz == 1))
+    def _():
+        zp_copy(1, 0, (d - 1, o)).start()
 
     def z_upper(s):
         @pl.loop(0, 4)
@@ -599,24 +612,39 @@
         zp_copy(1, 0, other_chip).wait_recv()
         zp_copy(1, 1, other_chip).wait_recv()
 
-    for s in (0, 1):
-        z_upper(s)
+    def upper_rows(s):
         for half in (0, 1):
             when(has_upper["x"], lambda: tx_copy(s, half).wait_recv())
         shift_x(s)
         half_rows(s, (0, 6, 12))
 
+    z_upper(0)
+    while early:
+        arrived(*early.pop(0))
+    leave(2)
+    out_copy = pltpu.make_async_copy(inp, out_hbm.at[:, 0], out_sem)
+    out_copy.start()
+    upper_rows(0)
+    z_upper(1)
+    upper_rows(1)
+
     for s in (0, 1):
         for c in range(4):
             for r in range(3):
                 core_copy(s, c, r).wait_recv()
 
     def grams(rows):
+        def halves(ref, x):
+            v = jnp.concatenate([flat(ref[s, x, rows]) for s in (0, 1)], axis=0)
+            hi = v.astype(BF16)
+            return hi, (v - hi.astype(F32)).astype(BF16)
+
         def body(x, total):
-            mine = [flat(pf[s, x, rows]) for s in (0, 1)]
-            left = jnp.concatenate(mine + [flat(ocp[s, x, rows]) for s in (0, 1)], axis=0)
-            right = jnp.concatenate(mine + [flat(hp[s, x, rows]) for s in (0, 1)], axis=0)
-            return total + gram(left, right)
+            (mh, ml), (oh, ol), (hh, hl) = halves(pf, x), halves(ocp, x), halves(hp, x)
+            left = jnp.concatenate([mh, oh, ml, ol], axis=0)
+            right = jnp.concatenate([mh, hh, ml, hl], axis=0)
+            full = lax.dot_general(left, right, (((1,), (1,)), ((), ())), preferred_element_type=F32)
+            return total + ((full[:32, :32] + full[32:, :32]) + (full[:32, 32:] + full[32:, 32:]))
         return body
 
     total = lax.fori_loop(0, 16, grams(pl.ds(0, 18)), jnp.zeros((32, 32), F32))
@@ -686,7 +714,8 @@
             when(by == 3 * side, lambda: passing(q, side).wait_send())
     for n, buf in ((0, e0), (1, e1)):
         for side in (0, 1):
-            when(sends("x", side), lambda: x_copy(n, buf, side).wait_send())
+            for r in range(3):
+                when(sends("x", side), lambda: x_copy(n, buf, side, r).wait_send())
         for part_ in (0, 1):
             for copy in z_copies(n, part_):
                 copy.wait_send()
@@ -719,7 +748,7 @@
         in_specs=[pl.BlockSpec(memory_space=pl.ANY)] * 2 + [pl.BlockSpec(memory_space=pltpu.VMEM)],
         out_specs=(pl.BlockSpec(memory_space=pl.ANY),) + (pl.BlockSpec(memory_space=pltpu.VMEM),) * 2,
         scratch_shapes=[
-            vm(NO, NX, NY, NZ), vm(NX, NY, NZ), vm(*field), vm(*field), vm(*field),
+            vm(NO, NX, NY, NZ), vm(NX, NY, NZ), vm(*field), vm(*field), vm(NX, NY, 8, 128),
             vm(NX, NY, 8, 128), vm(NX, NY, 8, 128),
             vm(2, 2, NY, 8, 128), vm(2, 2, NY, 8, 128), vm(2, 4, CHUNK, HALO, 8, 128),
             vm(2, 16 + HALO, NY + HALO, 8, 128), vm(16, NY, 8, 128), vm(2, 16, NY, 8, 128),
@@ -727,7 +756,7 @@
             vm(2, 2, NY, 8, 128), vm(2, 2, NY, 8, 128),
             vm(32, 128), vm(8, 16, 128), vm(16, 16, 128),
             dma(4), pltpu.SemaphoreType.DMA, pltpu.SemaphoreType.DMA,
-            dma(2, 8, 2), dma(2, 8, 2), dma(2, 4), dma(2, 4), dma(2, 4), dma(2, 2), dma(2, 2), dma(2, 3), dma(2, 3),
+            dma(2, 8, 2), dma(2, 8, 2), dma(2, 4), dma(2, 4), dma(2, 4), dma(2, 2, 3), dma(2, 2, 3), dma(2, 3), dma(2, 3),
             dma(2, 4, 3), dma(2, 4, 3), dma(4, 3), dma(4, 3),
             dma(2, 4), dma(2, 4), dma(2, 3), dma(2, 3), dma(2), dma(2),
             dma(7), dma(8), dma(15), dma(16),

time: 148 us -> 140 us (0.946)
  Pallas kernels: 143 us -> 135 us
    pallas_call x1, Pallas kernels: 143 us -> 135 us  [shards(): pl.pallas_call(kernel, out_shape=(jax.ShapeDtypeStruct((NO, 1, NX, NY, NZ...]
where the time goes in v4:
time: 140 us
  Pallas kernels  135 us (96%)
  local copies, waits for them, and re-layouts  5.01 us (4%)
    pallas_call x1, Pallas kernels, shards(): pl.pallas_call(kernel, out_shape=(jax.ShapeDtypeStruct((NO, 1, NX, NY, NZ...  135 us
    unnamed x7, local copies, waits for them, and re-layouts  5.01 us

profile of v4, /device:TPU:1, one launch (start us, length us, event | category | flops | bytes accessed | tf_op | source)
XLA Modules:
  0.0 140.3 jit_solution(9773711174303799827)
XLA Ops:
  0.6 134.6 %filter_and_subspace.1 = (f32[8,1,32,24,128]{4,3,2,1,0:T(8,128)}, f32[32,32]{1,0:T(8,128)}, f32[32,32]{1,0:T(8,128)}) custom-call(f32[8,1,32,24,128]{4,3,2,1,0:T(8,128)} %orb_hbm.1, f32[1,32,24,128]{3,2,1,0:T(8,128)} %pot_hbm.1, bf16[5,256,256]{2,1,0:T(8,128)(2,1)} %constant.2.clone.zmat_ref), custom_call_target="tpu_custom_call" | custom-call | tf_op jit(solution)/shard_map/filter_and_subspace/pallas_call | solution.py:741
  135.3 0.0 copy-start.1
  135.3 0.0 copy-start
  135.3 3.8 %copy.9 = f32[8,1,32,24,128]{4,3,2,1,0:T(8,128)} copy(f32[8,1,32,24,128]{4,3,2,1,0:T(8,128)} %get-tuple-element.6) | data formatting | bytes 6291456
  139.1 0.0 copy-done.1
  139.1 0.6 copy.10
  139.7 0.0 copy-done
  139.7 0.6 copy.11
Async XLA Ops:
  135.3 3.8 %copy-start.1 = (f32[32,32]{1,0:T(8,128)S(1)}, f32[32,32]{1,0:T(8,128)}, u32[]{:S(2)}) copy-start(f32[32,32]{1,0:T(8,128)} %get-tuple-element.7) | copy-start | bytes 12292
  135.3 4.4 %copy-start = (f32[32,32]{1,0:T(8,128)S(1)}, f32[32,32]{1,0:T(8,128)}, u32[]{:S(2)}) copy-start(f32[32,32]{1,0:T(8,128)} %get-tuple-element.8) | copy-start | bytes 12292

commit v5 on v4

--- a/solution.py
+++ b/solution.py
@@ -762,7 +762,7 @@
             dma(7), dma(8), dma(15), dma(16),
         ],
         compiler_params=pltpu.CompilerParams(
-            collective_id=0, has_side_effects=True, vmem_limit_bytes=58 * 2**20),
+            collective_id=0, has_side_effects=True, vmem_limit_bytes=47 * 2**20),
         name="filter_and_subspace",
     )(orbitals, potential, zmat)
     return out, cor, sub

time: 140 us -> 139 us (level)
  Pallas kernels: 135 us -> 133 us
    pallas_call x1, Pallas kernels: 135 us -> 133 us  [shards(): pl.pallas_call(kernel, out_shape=(jax.ShapeDtypeStruct((NO, 1, NX, NY, NZ...]
where the time goes in v5:
time: 139 us
  Pallas kernels  133 us (96%)
  local copies, waits for them, and re-layouts  4.95 us (4%)
    pallas_call x1, Pallas kernels, shards(): pl.pallas_call(kernel, out_shape=(jax.ShapeDtypeStruct((NO, 1, NX, NY, NZ...  133 us
    unnamed x7, local copies, waits for them, and re-layouts  4.95 us

profile of v5, /device:TPU:1, one launch (start us, length us, event | category | flops | bytes accessed | tf_op | source)
XLA Modules:
  0.0 138.8 jit_solution(4723307836751439293)
XLA Ops:
  0.6 0.0 copy-start
  0.6 1.1 copy-done
  1.7 0.0 copy-start.1
  1.7 1.0 copy-done.1
  2.7 133.2 %filter_and_subspace.1 = (f32[8,1,32,24,128]{4,3,2,1,0:T(8,128)S(1)}, f32[32,32]{1,0:T(8,128)S(1)}, f32[32,32]{1,0:T(8,128)S(1)}) custom-call(f32[8,1,32,24,128]{4,3,2,1,0:T(8,128)} %orb_hbm.1, f32[1,32,24,128]{3,2,1,0:T(8,128)S(1)} %copy-done.1, bf16[5,256,256]{2,1,0:T(8,128)(2,1)S(1)} %copy-done), custom_call_target="tpu_custom_call" | custom-call | tf_op jit(solution)/shard_map/filter_and_subspace/pallas_call | solution.py:741
  135.9 1.7 %copy.9 = f32[8,1,32,24,128]{4,3,2,1,0:T(8,128)} copy(f32[8,1,32,24,128]{4,3,2,1,0:T(8,128)S(1)} %get-tuple-element.6) | data formatting | bytes 6291456
  137.6 0.6 copy.10
  138.2 0.6 copy.11
Async XLA Ops:
  0.6 1.1 copy-start
  1.7 1.0 copy-start.1

commit v6 on v5

--- a/solution.py
+++ b/solution.py
@@ -412,6 +412,7 @@
     stage_rows(NX - HALO, NX, (6, 12), *first)
     send_x(1, e1, 0, 0)
     send_x(1, e1, 1, 0)
+    pump(5)
     pack_z(1, e1, 0)
     z_own(e1, 0)
     z_halo(0, 1)
@@ -424,8 +425,10 @@
             high = jnp.where(lane < 64, pltpu.roll(one, 64, axis=1), two)
             potp[x, y] = jnp.where(is_a, low, high)
 
+    pump(6)
     wait_x(0, e0, 1)
     z_halo(1, 0)
+    pump(7)
     wait_x(1, e1, 0)
 
     def pack_rows(lo, hi, rows):
@@ -535,7 +538,9 @@
                     inp[orb, at] = e2[at, :, orb]
 
     pack_z(1, e1, 1)
+    pump(12, 7)
     z_own(e1, 1)
+    pump(13, 7)
     wait_x(1, e1, 1)
     z_halo(1, 1)
     early = [(3, 0), (2, 0), (0, 0), (1, 0), (0, 1), (0, 2), (1, 1), (1, 2), (3, 1), (3, 2), (2, 1), (2, 2)]

time: 139 us -> 136 us (0.978)
  Pallas kernels: 133 us -> 130 us
    pallas_call x1, Pallas kernels: 133 us -> 130 us  [shards(): pl.pallas_call(kernel, out_shape=(jax.ShapeDtypeStruct((NO, 1, NX, NY, NZ...]
where the time goes in v6:
time: 136 us; the launch traced here: 135 us
  Pallas kernels  130 us (96%)
  local copies, waits for them, and re-layouts  4.95 us (4%)
    pallas_call x1, Pallas kernels, shards(): pl.pallas_call(kernel, out_shape=(jax.ShapeDtypeStruct((NO, 1, NX, NY, NZ...  130 us
    unnamed x7, local copies, waits for them, and re-layouts  4.95 us

profile of v6, /device:TPU:1, one launch (start us, length us, event | category | flops | bytes accessed | tf_op | source)
XLA Modules:
  0.0 135.3 jit_solution(5764619336918407343)
XLA Ops:
  0.6 0.0 copy-start
  0.6 1.1 copy-done
  1.7 0.0 copy-start.1
  1.7 1.0 copy-done.1
  2.7 129.7 %filter_and_subspace.1 = (f32[8,1,32,24,128]{4,3,2,1,0:T(8,128)S(1)}, f32[32,32]{1,0:T(8,128)S(1)}, f32[32,32]{1,0:T(8,128)S(1)}) custom-call(f32[8,1,32,24,128]{4,3,2,1,0:T(8,128)} %orb_hbm.1, f32[1,32,24,128]{3,2,1,0:T(8,128)S(1)} %copy-done.1, bf16[5,256,256]{2,1,0:T(8,128)(2,1)S(1)} %copy-done), custom_call_target="tpu_custom_call" | custom-call | tf_op jit(solution)/shard_map/filter_and_subspace/pallas_call | solution.py:746
  132.4 1.7 %copy.9 = f32[8,1,32,24,128]{4,3,2,1,0:T(8,128)} copy(f32[8,1,32,24,128]{4,3,2,1,0:T(8,128)S(1)} %get-tuple-element.6) | data formatting | bytes 6291456
  134.1 0.6 copy.10
  134.7 0.6 copy.11
Async XLA Ops:
  0.6 1.1 copy-start
  1.7 1.0 copy-start.1

commit v7 on v6

--- a/solution.py
+++ b/solution.py
@@ -623,6 +623,8 @@
         shift_x(s)
         half_rows(s, (0, 6, 12))
 
+    for _ in range(2):
+        arrived(*early.pop(0))
     z_upper(0)
     while early:
         arrived(*early.pop(0))

time: 136 us -> 135 us (level)
  no operation moved by 1% of the time
where the time goes in v7:
time: 135 us
  Pallas kernels  130 us (96%)
  local copies, waits for them, and re-layouts  4.95 us (4%)
    pallas_call x1, Pallas kernels, shards(): pl.pallas_call(kernel, out_shape=(jax.ShapeDtypeStruct((NO, 1, NX, NY, NZ...  130 us
    unnamed x7, local copies, waits for them, and re-layouts  4.95 us

profile of v7, /device:TPU:1, one launch (start us, length us, event | category | flops | bytes accessed | tf_op | source)
XLA Modules:
  0.0 135.1 jit_solution(13900416802909749715)
XLA Ops:
  0.6 0.0 copy-start
  0.6 1.1 copy-done
  1.7 0.0 copy-start.1
  1.7 1.0 copy-done.1
  2.7 129.5 %filter_and_subspace.1 = (f32[8,1,32,24,128]{4,3,2,1,0:T(8,128)S(1)}, f32[32,32]{1,0:T(8,128)S(1)}, f32[32,32]{1,0:T(8,128)S(1)}) custom-call(f32[8,1,32,24,128]{4,3,2,1,0:T(8,128)} %orb_hbm.1, f32[1,32,24,128]{3,2,1,0:T(8,128)S(1)} %copy-done.1, bf16[5,256,256]{2,1,0:T(8,128)(2,1)S(1)} %copy-done), custom_call_target="tpu_custom_call" | custom-call | tf_op jit(solution)/shard_map/filter_and_subspace/pallas_call | solution.py:748
  132.2 1.7 %copy.9 = f32[8,1,32,24,128]{4,3,2,1,0:T(8,128)} copy(f32[8,1,32,24,128]{4,3,2,1,0:T(8,128)S(1)} %get-tuple-element.6) | data formatting | bytes 6291456
  133.9 0.6 copy.10
  134.5 0.6 copy.11
Async XLA Ops:
  0.6 1.1 copy-start
  1.7 1.0 copy-start.1
